TPU v7x, 128 devices: a whole 4x4x4 slice. The times are simulated.
128 devices in a mesh: gx: 8 (over y, core), gy: 16 (over x, z).
Axes of the slice: x: 4, y: 4, z: 4, core: 2. Of those that a mesh axis runs over, the one named last changes fastest.
Arguments:
- positions: float32 [3, 2097152], P(None, ('gx', 'gy')), may hold values from 0 to 4
- charges: float32 [2097152], P(('gx', 'gy')), may hold values from -6 to 6
- counts: int32 [16384], P(('gx', 'gy')), may hold values from 1 to 128
- centres: float32 [3, 16384], P(None, ('gx', 'gy')), may hold values from 0 to 4
- freqs: float32 [3, 256], replicated, may hold values from -4 to 4
- phases: float32 [256], replicated, may hold values from -3.140625 to 3.140625
- m2m: bfloat16 [8, 256, 256], replicated, may hold values from -0.125 to 0.125
- m2l: bfloat16 [64, 256, 256], replicated, may hold values from -0.02734375 to 0.02734375
- send_nodes: int32 [128, 16, 32], P(('gx', 'gy')), may hold values from 0 to 143
- v_source: int32 [16384, 189], P(('gx', 'gy')), may hold values from 0 to 655
- v_offset: int32 [16384, 189], P(('gx', 'gy')), may hold values from 0 to 63
- u_source: int32 [16384, 27], P(('gx', 'gy')), may hold values from 0 to 383
Outputs:
- potential: float32 [2097152], P(('gx', 'gy'))
All inputs are finite; a program needn't handle non-finite values.
Results may differ from a plain program's by a relative error of at most 0.0027.
Values may be sent and summed in bfloat16 or wider, within the bound.
No kernel may reach another device: no remote copies, remote signals or barrier semaphores. Data moves between devices by JAX's collectives and lax.ppermute only.
A program may use at most 128 MiB of HBM per device.

v0:
```python
import jax
import jax.numpy as jnp
from jax import lax
from jax.sharding import PartitionSpec as P

MP = 256
LEAF_SIZE = 128
OFFSETS = 64
ULIST = 27
HALO = 128


def shifted(value, axis, by):
    devices = lax.axis_size(axis)
    pairs = [(i, i + by) for i in range(devices) if 0 <= i + by < devices]
    return lax.ppermute(value, axis, pairs)


def extended(value, sides, width):
    for axis, dim in sides:
        devices, length = (lax.axis_size(axis), value.shape[dim])
        up = [(i, (i + 1) % devices) for i in range(devices - 1)]
        down = [(j, i) for i, j in up]
        last = lax.slice_in_dim(value, length - width, length, axis=dim)
        first = lax.slice_in_dim(value, 0, width, axis=dim)
        before = lax.ppermute(last, axis, up)
        after = lax.ppermute(first, axis, down)
        value = jnp.concatenate([before, value, after], axis=dim)
    return value


def basis_of(rel, freqs, phases):
    angle = jnp.einsum("cln,ck->lnk", rel, freqs, precision=lax.Precision.HIGHEST) + phases
    return jnp.cos(angle)


def near_field(spots, widened, u_list):
    leaves = spots.shape[1]
    groups = leaves // 8
    slot_ids = jnp.arange(LEAF_SIZE)

    def group_fn(args):
        here, lists, leaf_ids = args
        source = widened[:, lists]
        diff = here[:, :, :, None, None] - source[:3, :, None, :, :]
        dist2 = jnp.sum(diff * diff, axis=0)
        own = lists[:, None, :, None] == (HALO + leaf_ids)[:, None, None, None]
        same = slot_ids[None, :, None, None] == slot_ids[None, None, None, :]
        term = source[3][:, None, :, :] / jnp.sqrt(dist2 + 0.01)
        term = jnp.where(own & same, jnp.float32(0.0), term)
        return jnp.sum(term, axis=(2, 3)) * (ULIST * LEAF_SIZE) ** (-0.5)

    here_g = spots.reshape(3, groups, 8, LEAF_SIZE).transpose(1, 0, 2, 3)
    lists_g = u_list.reshape(groups, 8, ULIST)
    ids_g = jnp.arange(leaves, dtype=jnp.int32).reshape(groups, 8)
    out = lax.map(group_fn, (here_g, lists_g, ids_g))
    return out.reshape(leaves, LEAF_SIZE)


def per_device(
    positions,
    charges,
    counts,
    centres,
    freqs,
    phases,
    m2m,
    m2l,
    send_nodes,
    v_source,
    v_offset,
    u_source,
):
    leaves = counts.shape[0]
    shift_count = send_nodes.shape[1]
    per_peer = send_nodes.shape[2]
    reach = shift_count // 2
    live = (jnp.arange(LEAF_SIZE, dtype=jnp.int32)[None, :] < counts[:, None]).astype(jnp.float32)
    charge = charges.reshape(leaves, LEAF_SIZE) * live
    spots = positions.reshape(3, leaves, LEAF_SIZE)
    basis = basis_of(spots - centres[:, :, None], freqs, phases)
    leaf_mult = (
        jnp.einsum("ln,lnk->lk", charge, basis, precision=lax.Precision.HIGHEST)
        * LEAF_SIZE ** (-0.5)
    ).astype(jnp.bfloat16)
    parent = jnp.einsum(
        "pck,ckj->pj",
        leaf_mult.reshape(leaves // 8, 8, MP),
        m2m,
        preferred_element_type=jnp.float32,
    ).astype(jnp.bfloat16)
    nodes = jnp.concatenate([leaf_mult, parent], axis=0)
    outgoing = nodes[send_nodes[0]]
    arrived_parts = []
    for index in range(shift_count):
        offset = index + 1 if index < reach else reach - 1 - index
        arrived_parts.append(shifted(outgoing[index], ("gx", "gy"), offset))
    arrived = jnp.stack(arrived_parts, axis=0)
    table = jnp.concatenate([nodes, arrived.reshape(shift_count * per_peer, MP)], axis=0)
    stacked = jnp.concatenate([positions, charge.reshape(1, leaves * LEAF_SIZE)], axis=0)
    widened = extended(stacked, ((("gx", "gy"), 1),), HALO * LEAF_SIZE)
    widened = widened.reshape(4, leaves + 2 * HALO, LEAF_SIZE)
    gathered = table[v_source]
    onehot = (v_offset[:, :, None] == jnp.arange(OFFSETS, dtype=jnp.int32)[None, None, :]).astype(
        jnp.bfloat16
    )
    summed = jnp.einsum(
        "lvo,lvk->lok", onehot, gathered, preferred_element_type=jnp.float32
    ).astype(jnp.bfloat16)
    local = jnp.dot(
        summed.reshape(leaves, OFFSETS * MP),
        m2l.reshape(OFFSETS * MP, MP),
        preferred_element_type=jnp.float32,
    )
    far = jnp.einsum("lnk,lk->ln", basis, local, precision=lax.Precision.HIGHEST) * MP ** (-0.5)
    near = near_field(spots, widened, u_source)
    return ((far + near) * live).reshape(leaves * LEAF_SIZE)


def solution(mesh):
    in_specs = (
        P(None, ("gx", "gy")),
        P(("gx", "gy")),
        P(("gx", "gy")),
        P(None, ("gx", "gy")),
        P(),
        P(),
        P(),
        P(),
        P(("gx", "gy"), None, None),
        P(("gx", "gy"), None),
        P(("gx", "gy"), None),
        P(("gx", "gy"), None),
    )
    out_specs = P(("gx", "gy"))
    return jax.shard_map(
        per_device, mesh=mesh, in_specs=in_specs, out_specs=out_specs, check_vma=False
    )
```

profile of v0, /device:TPU:10, one launch (start us, length us, event | category | flops | bytes accessed | tf_op | source)
XLA Modules:
  0.0 750.4 jit_solution(16629760491441276399)
XLA Ops:
  11.8 17.3 %fusion.14 = f32[128,128,256]{2,1,0:T(8,128)S(1)} fusion(f32[3,16384]{1,0:T(4,128)} %param.14, f32[3,128]{0,1:T(8,128)S(1)} %copy.40, f32[3,256]{1,0:T(4,128)} %param.18), kind=kOutput, calls=%fused_computation.34 | convolution fusion | flops 151044096 | bytes 16978432 | tf_op jit(solution)/shard_map/cln,ck->lnk/dot_general | solution.py:33
  34.9 70.5 %fusion.5 = f32[128,1,256]{2,1,0:T(1,128)S(1)} fusion(f32[128,128,1]{1,2,0:T(1,128)S(1)} %bitcast.140, f32[128,128,256]{2,1,0:T(8,128)S(1)} %fusion.14, f32[256]{0:T(256)S(1)} %copy-done.6), kind=kOutput, calls=%fused_computation.18 | convolution fusion | flops 54525952 | bytes 16974848 | tf_op jit(solution)/shard_map/ln,lnk->lk/dot_general | solution.py:83
  172.3 67.6 %gather_fusion.2 = bf16[24192,256]{1,0:T(8,128)(2,1)} fusion(bf16[656,256]{1,0:T(8,128)(2,1)S(1)} %pad_maximum_fusion, s32[24576]{0:T(1024)S(1)} %pad_clamp_fusion.1), kind=kCustom, calls=%fused_computation.2 | custom fusion | bytes 24869376 | tf_op jit(solution)/shard_map/gather | solution.py:103
  239.9 16.3 %reshape.210 = bf16[128,189,256]{2,1,0:T(8,128)(2,1)} reshape(bf16[24192,256]{1,0:T(8,128)(2,1)} %gather_fusion.2) | data formatting | bytes 24772608 | tf_op jit(solution)/shard_map/gather | solution.py:103
  262.7 9.2 %fusion.9 = f32[128,256,1]{1,0,2:T(8,128)S(1)} fusion(bf16[64,256,256]{2,1,0:T(8,128)(2,1)} %param.21, bf16[128,64,256]{2,1,0:T(8,128)(2,1)S(1)} %fusion.12), kind=kOutput, calls=%fused_computation.23 | convolution fusion | flops 1073741824 | bytes 12713984 | tf_op jit(solution)/shard_map/dot_general | solution.py:110
  272.0 69.7 %fusion.4 = f32[128,1,128]{2,1,0:T(1,128)S(1)} fusion(f32[128,128,256]{2,1,0:T(8,128)S(1)} %bitcast.131, f32[256]{0:T(256)S(1)} %copy-done.6, f32[128,256,1]{1,0,2:T(8,128)S(1)} %fusion.9), kind=kOutput, calls=%fused_computation.17 | convolution fusion | flops 54525952 | bytes 16974848 | tf_op jit(solution)/shard_map/lnk,lk->ln/dot_general | solution.py:115
  341.9 407.0 %while.11 = (s32[]{:T(128)}, f32[16,8,128]{2,1,0:T(8,128)S(1)}, s32[16,8,27]{2,1,0:T(8,128)S(1)}, s32[16,8]{1,0:T(8,128)S(1)}, f32[4,384,128]{2,0,1:T(4,128)S(1)}, /*index=5*/f32[16,3,8,128]{3,2,0,1:T(8,128)S(1)}, s32[]{:T(128)}) while((s32[]{:T(128)}, f32[16,8,128]{2,1,0:T(8,128)S(1)}, s32[16,8,27]{2,1,0:T(8,128)S(1)}, ...), condition=%wide.region_3.4_spmd.clone, body=%wide.region_0.3_spmd.clone.sunk | while | flops 46024552 | bytes 30837264 | solution.py:56
  343.1 16.8 %multiply_reduce_fusion.2 = f32[8,128,27,128]{3,1,2,0:T(8,128)} fusion(f32[3,8,27,128]{3,2,1,0:T(8,128)S(1)} %copy.71, f32[3,8,128]{2,1,0:T(8,128)S(1)} %dynamic-slice_bitcast_fusion.2), kind=kLoop, calls=%fused_computation.4.clone.1 | loop fusion | flops 28311552 | bytes 14499840 | tf_op jit(solution)/shard_map/while/body/eval_jaxpr/reduce_sum | solution.py:46
  360.1 7.2 select_reduce_fusion.2
  368.5 16.8 %multiply_reduce_fusion.2 = f32[8,128,27,128]{3,1,2,0:T(8,128)} fusion(f32[3,8,27,128]{3,2,1,0:T(8,128)S(1)} %copy.71, f32[3,8,128]{2,1,0:T(8,128)S(1)} %dynamic-slice_bitcast_fusion.2), kind=kLoop, calls=%fused_computation.4.clone.1 | loop fusion | flops 28311552 | bytes 14499840 | tf_op jit(solution)/shard_map/while/body/eval_jaxpr/reduce_sum | solution.py:46
  385.6 7.2 select_reduce_fusion.2
  393.9 16.8 %multiply_reduce_fusion.2 = f32[8,128,27,128]{3,1,2,0:T(8,128)} fusion(f32[3,8,27,128]{3,2,1,0:T(8,128)S(1)} %copy.71, f32[3,8,128]{2,1,0:T(8,128)S(1)} %dynamic-slice_bitcast_fusion.2), kind=kLoop, calls=%fused_computation.4.clone.1 | loop fusion | flops 28311552 | bytes 14499840 | tf_op jit(solution)/shard_map/while/body/eval_jaxpr/reduce_sum | solution.py:46
  411.0 7.2 select_reduce_fusion.2
  419.4 16.8 %multiply_reduce_fusion.2 = f32[8,128,27,128]{3,1,2,0:T(8,128)} fusion(f32[3,8,27,128]{3,2,1,0:T(8,128)S(1)} %copy.71, f32[3,8,128]{2,1,0:T(8,128)S(1)} %dynamic-slice_bitcast_fusion.2), kind=kLoop, calls=%fused_computation.4.clone.1 | loop fusion | flops 28311552 | bytes 14499840 | tf_op jit(solution)/shard_map/while/body/eval_jaxpr/reduce_sum | solution.py:46
  436.4 7.2 select_reduce_fusion.2
  444.8 16.8 %multiply_reduce_fusion.2 = f32[8,128,27,128]{3,1,2,0:T(8,128)} fusion(f32[3,8,27,128]{3,2,1,0:T(8,128)S(1)} %copy.71, f32[3,8,128]{2,1,0:T(8,128)S(1)} %dynamic-slice_bitcast_fusion.2), kind=kLoop, calls=%fused_computation.4.clone.1 | loop fusion | flops 28311552 | bytes 14499840 | tf_op jit(solution)/shard_map/while/body/eval_jaxpr/reduce_sum | solution.py:46
  461.9 7.2 select_reduce_fusion.2
  470.2 16.8 %multiply_reduce_fusion.2 = f32[8,128,27,128]{3,1,2,0:T(8,128)} fusion(f32[3,8,27,128]{3,2,1,0:T(8,128)S(1)} %copy.71, f32[3,8,128]{2,1,0:T(8,128)S(1)} %dynamic-slice_bitcast_fusion.2), kind=kLoop, calls=%fused_computation.4.clone.1 | loop fusion | flops 28311552 | bytes 14499840 | tf_op jit(solution)/shard_map/while/body/eval_jaxpr/reduce_sum | solution.py:46
  487.3 7.2 select_reduce_fusion.2
  495.7 16.8 %multiply_reduce_fusion.2 = f32[8,128,27,128]{3,1,2,0:T(8,128)} fusion(f32[3,8,27,128]{3,2,1,0:T(8,128)S(1)} %copy.71, f32[3,8,128]{2,1,0:T(8,128)S(1)} %dynamic-slice_bitcast_fusion.2), kind=kLoop, calls=%fused_computation.4.clone.1 | loop fusion | flops 28311552 | bytes 14499840 | tf_op jit(solution)/shard_map/while/body/eval_jaxpr/reduce_sum | solution.py:46
  512.7 7.2 select_reduce_fusion.2
  521.1 16.8 %multiply_reduce_fusion.2 = f32[8,128,27,128]{3,1,2,0:T(8,128)} fusion(f32[3,8,27,128]{3,2,1,0:T(8,128)S(1)} %copy.71, f32[3,8,128]{2,1,0:T(8,128)S(1)} %dynamic-slice_bitcast_fusion.2), kind=kLoop, calls=%fused_computation.4.clone.1 | loop fusion | flops 28311552 | bytes 14499840 | tf_op jit(solution)/shard_map/while/body/eval_jaxpr/reduce_sum | solution.py:46
  538.2 7.2 select_reduce_fusion.2
  546.5 16.8 %multiply_reduce_fusion.2 = f32[8,128,27,128]{3,1,2,0:T(8,128)} fusion(f32[3,8,27,128]{3,2,1,0:T(8,128)S(1)} %copy.71, f32[3,8,128]{2,1,0:T(8,128)S(1)} %dynamic-slice_bitcast_fusion.2), kind=kLoop, calls=%fused_computation.4.clone.1 | loop fusion | flops 28311552 | bytes 14499840 | tf_op jit(solution)/shard_map/while/body/eval_jaxpr/reduce_sum | solution.py:46
  572.0 16.8 %multiply_reduce_fusion.2 = f32[8,128,27,128]{3,1,2,0:T(8,128)} fusion(f32[3,8,27,128]{3,2,1,0:T(8,128)S(1)} %copy.71, f32[3,8,128]{2,1,0:T(8,128)S(1)} %dynamic-slice_bitcast_fusion.2), kind=kLoop, calls=%fused_computation.4.clone.1 | loop fusion | flops 28311552 | bytes 14499840 | tf_op jit(solution)/shard_map/while/body/eval_jaxpr/reduce_sum | solution.py:46
  597.4 16.8 %multiply_reduce_fusion.2 = f32[8,128,27,128]{3,1,2,0:T(8,128)} fusion(f32[3,8,27,128]{3,2,1,0:T(8,128)S(1)} %copy.71, f32[3,8,128]{2,1,0:T(8,128)S(1)} %dynamic-slice_bitcast_fusion.2), kind=kLoop, calls=%fused_computation.4.clone.1 | loop fusion | flops 28311552 | bytes 14499840 | tf_op jit(solution)/shard_map/while/body/eval_jaxpr/reduce_sum | solution.py:46
  622.8 16.8 %multiply_reduce_fusion.2 = f32[8,128,27,128]{3,1,2,0:T(8,128)} fusion(f32[3,8,27,128]{3,2,1,0:T(8,128)S(1)} %copy.71, f32[3,8,128]{2,1,0:T(8,128)S(1)} %dynamic-slice_bitcast_fusion.2), kind=kLoop, calls=%fused_computation.4.clone.1 | loop fusion | flops 28311552 | bytes 14499840 | tf_op jit(solution)/shard_map/while/body/eval_jaxpr/reduce_sum | solution.py:46
  648.3 16.8 %multiply_reduce_fusion.2 = f32[8,128,27,128]{3,1,2,0:T(8,128)} fusion(f32[3,8,27,128]{3,2,1,0:T(8,128)S(1)} %copy.71, f32[3,8,128]{2,1,0:T(8,128)S(1)} %dynamic-slice_bitcast_fusion.2), kind=kLoop, calls=%fused_computation.4.clone.1 | loop fusion | flops 28311552 | bytes 14499840 | tf_op jit(solution)/shard_map/while/body/eval_jaxpr/reduce_sum | solution.py:46
  673.7 16.8 %multiply_reduce_fusion.2 = f32[8,128,27,128]{3,1,2,0:T(8,128)} fusion(f32[3,8,27,128]{3,2,1,0:T(8,128)S(1)} %copy.71, f32[3,8,128]{2,1,0:T(8,128)S(1)} %dynamic-slice_bitcast_fusion.2), kind=kLoop, calls=%fused_computation.4.clone.1 | loop fusion | flops 28311552 | bytes 14499840 | tf_op jit(solution)/shard_map/while/body/eval_jaxpr/reduce_sum | solution.py:46
  699.2 16.8 %multiply_reduce_fusion.2 = f32[8,128,27,128]{3,1,2,0:T(8,128)} fusion(f32[3,8,27,128]{3,2,1,0:T(8,128)S(1)} %copy.71, f32[3,8,128]{2,1,0:T(8,128)S(1)} %dynamic-slice_bitcast_fusion.2), kind=kLoop, calls=%fused_computation.4.clone.1 | loop fusion | flops 28311552 | bytes 14499840 | tf_op jit(solution)/shard_map/while/body/eval_jaxpr/reduce_sum | solution.py:46
  716.2 7.2 select_reduce_fusion.2
  724.6 16.8 %multiply_reduce_fusion.2 = f32[8,128,27,128]{3,1,2,0:T(8,128)} fusion(f32[3,8,27,128]{3,2,1,0:T(8,128)S(1)} %copy.71, f32[3,8,128]{2,1,0:T(8,128)S(1)} %dynamic-slice_bitcast_fusion.2), kind=kLoop, calls=%fused_computation.4.clone.1 | loop fusion | flops 28311552 | bytes 14499840 | tf_op jit(solution)/shard_map/while/body/eval_jaxpr/reduce_sum | solution.py:46
  (306 shorter events, 163.5 us)
Async XLA Ops:
  0.0 105.6 %copy-start = (bf16[8,256,256]{2,1,0:T(8,128)(2,1)S(1)}, bf16[8,256,256]{2,1,0:T(8,128)(2,1)}, u32[]{:S(2)}) copy-start(bf16[8,256,256]{2,1,0:T(8,128)(2,1)} %param.20) | copy-start | bytes 3145732
  0.0 34.9 %copy-start.6 = (f32[256]{0:T(256)S(1)}, f32[256]{0:T(256)}, u32[]{:S(2)}) copy-start(f32[256]{0:T(256)} %param.19) | copy-start | bytes 3076
  2.1 339.6 %collective-permute-start.16 = (f32[4,16384]{1,0:T(4,128)S(1)}, f32[4,16384]{1,0:T(4,128)S(1)}, u32[]{:S(2)}, u32[]{:S(2)}) collective-permute-start(f32[4,16384]{1,0:T(4,128)S(1)} %pad_maximum_fusion.1), channel_id=1, source_target_pairs={{0,1},{1,2},{2,3},{3,4},{4,5},{5,6},{6,7},{7,8},{8,9},{9,10},{10,1... | collective-permute-start | bytes 786440 | tf_op jit(solution)/shard_map/ppermute | solution.py:26
  5.9 335.7 %collective-permute-start.17 = (f32[4,16384]{1,0:T(4,128)S(1)}, f32[4,16384]{1,0:T(4,128)S(1)}, u32[]{:S(2)}, u32[]{:S(2)}) collective-permute-start(f32[4,16384]{1,0:T(4,128)S(1)} %pad_maximum_fusion.1), channel_id=1, source_target_pairs={{1,0},{2,1},{3,2},{4,3},{5,4},{6,5},{7,6},{8,7},{9,8},{10,9},{11,1... | collective-permute-start | bytes 786440 | tf_op jit(solution)/shard_map/ppermute | solution.py:27
  29.1 5.8 copy-start.2
  29.1 76.4 %copy-start.8 = (s32[1,16,32]{2,1,0:T(8,128)S(1)}, s32[1,16,32]{2,1,0:T(8,128)}, u32[]{:S(2)}) copy-start(s32[1,16,32]{2,1,0:T(8,128)} %param.22) | copy-start | bytes 6148
  29.1 89.8 %copy-start.5 = (s32[128,189]{0,1:T(8,128)S(1)}, s32[128,189]{0,1:T(8,128)}, u32[]{:S(2)}) copy-start(s32[128,189]{0,1:T(8,128)} %param.23) | copy-start | bytes 290308
  29.1 90.3 %copy-start.4 = (s32[128,189]{0,1:T(8,128)S(1)}, s32[128,189]{0,1:T(8,128)}, u32[]{:S(2)}) copy-start(s32[128,189]{0,1:T(8,128)} %param.24) | copy-start | bytes 290308
  29.2 90.4 %copy-start.3 = (f32[3,16384]{1,0:T(4,128)S(1)}, f32[3,16384]{1,0:T(4,128)}, u32[]{:S(2)}) copy-start(f32[3,16384]{1,0:T(4,128)} %param.14) | copy-start | bytes 589828
  29.2 90.4 %copy-start.7 = (s32[128,27]{0,1:T(8,128)S(1)}, s32[128,27]{0,1:T(8,128)}, u32[]{:S(2)}) copy-start(s32[128,27]{0,1:T(8,128)} %param.25) | copy-start | bytes 41476
  107.9 11.9 %collective-permute-start = (bf16[32,256]{1,0:T(8,128)(2,1)S(1)}, bf16[32,256]{1,0:T(8,128)(2,1)S(1)}, u32[]{:S(2)}, u32[]{:S(2)}) collective-permute-start(bf16[32,256]{1,0:T(8,128)(2,1)S(1)} %get-tuple-element.102), channel_id=1, source_target_pairs={{0,1},{1,2},{2,3},{3,4},{4,5},{5,6},{6,7},{7,8},{8,9},{9,10},{10,1... | collective-permute-start | bytes 49160 | tf_op jit(solution)/shard_map/ppermute | solution.py:16
  109.8 13.1 %collective-permute-start.1 = (bf16[32,256]{1,0:T(8,128)(2,1)S(1)}, bf16[32,256]{1,0:T(8,128)(2,1)S(1)}, u32[]{:S(2)}, u32[]{:S(2)}) collective-permute-start(bf16[32,256]{1,0:T(8,128)(2,1)S(1)} %get-tuple-element.101), channel_id=1, source_target_pairs={{0,2},{1,3},{2,4},{3,5},{4,6},{5,7},{6,8},{7,9},{8,10},{9,11},{10,... | collective-permute-start | bytes 49160 | tf_op jit(solution)/shard_map/ppermute | solution.py:16
  115.1 11.2 %collective-permute-start.2 = (bf16[32,256]{1,0:T(8,128)(2,1)S(1)}, bf16[32,256]{1,0:T(8,128)(2,1)S(1)}, u32[]{:S(2)}, u32[]{:S(2)}) collective-permute-start(bf16[32,256]{1,0:T(8,128)(2,1)S(1)} %get-tuple-element.100), channel_id=1, source_target_pairs={{0,3},{1,4},{2,5},{3,6},{4,7},{5,8},{6,9},{7,10},{8,11},{9,12},{10... | collective-permute-start | bytes 49160 | tf_op jit(solution)/shard_map/ppermute | solution.py:16
  119.7 10.0 %collective-permute-start.3 = (bf16[32,256]{1,0:T(8,128)(2,1)S(1)}, bf16[32,256]{1,0:T(8,128)(2,1)S(1)}, u32[]{:S(2)}, u32[]{:S(2)}) collective-permute-start(bf16[32,256]{1,0:T(8,128)(2,1)S(1)} %get-tuple-element.99), channel_id=1, source_target_pairs={{0,4},{1,5},{2,6},{3,7},{4,8},{5,9},{6,10},{7,11},{8,12},{9,13},{1... | collective-permute-start | bytes 49160 | tf_op jit(solution)/shard_map/ppermute | solution.py:16
  122.9 13.4 %collective-permute-start.4 = (bf16[32,256]{1,0:T(8,128)(2,1)S(1)}, bf16[32,256]{1,0:T(8,128)(2,1)S(1)}, u32[]{:S(2)}, u32[]{:S(2)}) collective-permute-start(bf16[32,256]{1,0:T(8,128)(2,1)S(1)} %get-tuple-element.98), channel_id=1, source_target_pairs={{0,5},{1,6},{2,7},{3,8},{4,9},{5,10},{6,11},{7,12},{8,13},{9,14},{... | collective-permute-start | bytes 49160 | tf_op jit(solution)/shard_map/ppermute | solution.py:16
  126.2 14.3 %collective-permute-start.5 = (bf16[32,256]{1,0:T(8,128)(2,1)S(1)}, bf16[32,256]{1,0:T(8,128)(2,1)S(1)}, u32[]{:S(2)}, u32[]{:S(2)}) collective-permute-start(bf16[32,256]{1,0:T(8,128)(2,1)S(1)} %get-tuple-element.97), channel_id=1, source_target_pairs={{0,6},{1,7},{2,8},{3,9},{4,10},{5,11},{6,12},{7,13},{8,14},{9,15},... | collective-permute-start | bytes 49160 | tf_op jit(solution)/shard_map/ppermute | solution.py:16
  129.7 13.4 %collective-permute-start.6 = (bf16[32,256]{1,0:T(8,128)(2,1)S(1)}, bf16[32,256]{1,0:T(8,128)(2,1)S(1)}, u32[]{:S(2)}, u32[]{:S(2)}) collective-permute-start(bf16[32,256]{1,0:T(8,128)(2,1)S(1)} %get-tuple-element.96), channel_id=1, source_target_pairs={{0,7},{1,8},{2,9},{3,10},{4,11},{5,12},{6,13},{7,14},{8,15},{9,16}... | collective-permute-start | bytes 49160 | tf_op jit(solution)/shard_map/ppermute | solution.py:16
  136.2 9.3 %collective-permute-start.7 = (bf16[32,256]{1,0:T(8,128)(2,1)S(1)}, bf16[32,256]{1,0:T(8,128)(2,1)S(1)}, u32[]{:S(2)}, u32[]{:S(2)}) collective-permute-start(bf16[32,256]{1,0:T(8,128)(2,1)S(1)} %get-tuple-element.95), channel_id=1, source_target_pairs={{0,8},{1,9},{2,10},{3,11},{4,12},{5,13},{6,14},{7,15},{8,16},{9,17... | collective-permute-start | bytes 49160 | tf_op jit(solution)/shard_map/ppermute | solution.py:16
  140.5 10.9 %collective-permute-start.8 = (bf16[32,256]{1,0:T(8,128)(2,1)S(1)}, bf16[32,256]{1,0:T(8,128)(2,1)S(1)}, u32[]{:S(2)}, u32[]{:S(2)}) collective-permute-start(bf16[32,256]{1,0:T(8,128)(2,1)S(1)} %get-tuple-element.94), channel_id=1, source_target_pairs={{1,0},{2,1},{3,2},{4,3},{5,4},{6,5},{7,6},{8,7},{9,8},{10,9},{11,1... | collective-permute-start | bytes 49160 | tf_op jit(solution)/shard_map/ppermute | solution.py:16
  143.1 10.2 %collective-permute-start.9 = (bf16[32,256]{1,0:T(8,128)(2,1)S(1)}, bf16[32,256]{1,0:T(8,128)(2,1)S(1)}, u32[]{:S(2)}, u32[]{:S(2)}) collective-permute-start(bf16[32,256]{1,0:T(8,128)(2,1)S(1)} %get-tuple-element.93), channel_id=1, source_target_pairs={{2,0},{3,1},{4,2},{5,3},{6,4},{7,5},{8,6},{9,7},{10,8},{11,9},{12,... | collective-permute-start | bytes 49160 | tf_op jit(solution)/shard_map/ppermute | solution.py:16
  145.6 12.0 %collective-permute-start.10 = (bf16[32,256]{1,0:T(8,128)(2,1)S(1)}, bf16[32,256]{1,0:T(8,128)(2,1)S(1)}, u32[]{:S(2)}, u32[]{:S(2)}) collective-permute-start(bf16[32,256]{1,0:T(8,128)(2,1)S(1)} %get-tuple-element.92), channel_id=1, source_target_pairs={{3,0},{4,1},{5,2},{6,3},{7,4},{8,5},{9,6},{10,7},{11,8},{12,9},{13... | collective-permute-start | bytes 49160 | tf_op jit(solution)/shard_map/ppermute | solution.py:16
  151.4 9.2 %collective-permute-start.11 = (bf16[32,256]{1,0:T(8,128)(2,1)S(1)}, bf16[32,256]{1,0:T(8,128)(2,1)S(1)}, u32[]{:S(2)}, u32[]{:S(2)}) collective-permute-start(bf16[32,256]{1,0:T(8,128)(2,1)S(1)} %get-tuple-element.91), channel_id=1, source_target_pairs={{4,0},{5,1},{6,2},{7,3},{8,4},{9,5},{10,6},{11,7},{12,8},{13,9},{1... | collective-permute-start | bytes 49160 | tf_op jit(solution)/shard_map/ppermute | solution.py:16
  153.4 11.8 %collective-permute-start.12 = (bf16[32,256]{1,0:T(8,128)(2,1)S(1)}, bf16[32,256]{1,0:T(8,128)(2,1)S(1)}, u32[]{:S(2)}, u32[]{:S(2)}) collective-permute-start(bf16[32,256]{1,0:T(8,128)(2,1)S(1)} %get-tuple-element.90), channel_id=1, source_target_pairs={{5,0},{6,1},{7,2},{8,3},{9,4},{10,5},{11,6},{12,7},{13,8},{14,9},{... | collective-permute-start | bytes 49160 | tf_op jit(solution)/shard_map/ppermute | solution.py:16
  157.6 10.9 %collective-permute-start.13 = (bf16[32,256]{1,0:T(8,128)(2,1)S(1)}, bf16[32,256]{1,0:T(8,128)(2,1)S(1)}, u32[]{:S(2)}, u32[]{:S(2)}) collective-permute-start(bf16[32,256]{1,0:T(8,128)(2,1)S(1)} %get-tuple-element.89), channel_id=1, source_target_pairs={{6,0},{7,1},{8,2},{9,3},{10,4},{11,5},{12,6},{13,7},{14,8},{15,9},... | collective-permute-start | bytes 49160 | tf_op jit(solution)/shard_map/ppermute | solution.py:16
  160.6 7.9 %collective-permute-start.14 = (bf16[32,256]{1,0:T(8,128)(2,1)S(1)}, bf16[32,256]{1,0:T(8,128)(2,1)S(1)}, u32[]{:S(2)}, u32[]{:S(2)}) collective-permute-start(bf16[32,256]{1,0:T(8,128)(2,1)S(1)} %get-tuple-element.88), channel_id=1, source_target_pairs={{7,0},{8,1},{9,2},{10,3},{11,4},{12,5},{13,6},{14,7},{15,8},{16,9}... | collective-permute-start | bytes 49160 | tf_op jit(solution)/shard_map/ppermute | solution.py:16
  165.2 7.1 collective-permute-start.15
  256.2 15.7 %slice-start = ((s8[16777216]{0:T(1024)(128)(4,1)}), s8[4194304]{0:T(1024)(128)(4,1)S(1)}, s32[]{:S(2)}) async-start(s8[16777216]{0:T(1024)(128)(4,1)} %bitcast.130), calls=%async_computation | async-start | bytes 8388608
  256.2 15.7 %slice-start.1 = ((s8[16777216]{0:T(1024)(128)(4,1)}), s8[4194304]{0:T(1024)(128)(4,1)S(1)}, s32[]{:S(2)}) async-start(s8[16777216]{0:T(1024)(128)(4,1)} %bitcast.130), calls=%async_computation.1 | async-start | bytes 8388608
  256.2 15.7 %slice-start.2 = ((s8[16777216]{0:T(1024)(128)(4,1)}), s8[4194304]{0:T(1024)(128)(4,1)S(1)}, s32[]{:S(2)}) async-start(s8[16777216]{0:T(1024)(128)(4,1)} %bitcast.130), calls=%async_computation.2 | async-start | bytes 8388608
  262.7 9.2 %slice-start.3 = ((s8[16777216]{0:T(1024)(128)(4,1)}), s8[4194304]{0:T(1024)(128)(4,1)S(1)}, s32[]{:S(2)}) async-start(s8[16777216]{0:T(1024)(128)(4,1)} %bitcast.130), calls=%async_computation.3 | async-start | bytes 8388608
  341.9 407.0 %copy-start.9 = (s32[128]{0:T(128)S(1)}, s32[128]{0:T(128)}, u32[]{:S(2)}) copy-start(s32[128]{0:T(128)} %param.16) | copy-start | bytes 1540
  748.9 1.3 copy-start.1
where the time goes:
time: 762 us; the launch traced here: 750 us
  other arithmetic  391 us (51%)
  matrix products  173 us (23%)
  local copies, waits for them, and re-layouts  113 us (15%)
  starting transfers between devices  67.4 us (9%)
    reduce_sum x16, other arithmetic, group_fn(): dist2 = jnp.sum(diff * diff, axis=0)  269 us
    reduce_sum x16, other arithmetic, group_fn(): return jnp.sum(term, axis=(2, 3)) * (ULIST * LEAF_SIZE) ** (-0.5)  116 us
    gather x2, local copies, waits for them, and re-layouts, per_device(): gathered = table[v_source]  83.8 us
    dot_general x1, matrix products, per_device(): jnp.einsum('ln,lnk->lk', charge, basis, precision=lax.Precision.HIGHEST)  70.5 us
    dot_general x1, matrix products, per_device(): jnp.einsum('lnk,lk->ln', basis, local, precision=lax.Precision.HIGHEST)  69.7 us
    ppermute x16, starting transfers between devices, shifted(): return lax.ppermute(value, axis, pairs)  59.4 us
    dot_general x1, matrix products, basis_of(): jnp.einsum('cln,ck->lnk', rel, freqs, precision=lax.Precision.HIGHEST)  17.3 us
  transfers between devices with their start and end apart: 18, of which 1 were waited for; matrix products, arithmetic and copies ran while one was open for 35% of the time, Pallas kernels for 0%

commit v1 on v0

v1 whole, which is shorter than its diff:
```python
import math

import jax
import jax.numpy as jnp
import numpy as np
from jax import lax
from jax.experimental import pallas as pl
from jax.experimental.pallas import tpu as pltpu
from jax.sharding import PartitionSpec as P

F32 = jnp.float32
BF = jnp.bfloat16
MP = 256
LEAF = 128
OFFSETS = 64
VLIST = 189
ULIST = 27
CAP = 32
REACH = 8
SHIFTS = 16
AXES = ("gx", "gy")
ROWS = 256
MIB = 2**20
SM = pl.BlockSpec(memory_space=pltpu.SMEM)
VM = pl.BlockSpec(memory_space=pltpu.VMEM)
HBM = pl.BlockSpec(memory_space=pl.ANY)
NT = (((1,), (1,)), ((), ()))


def sine_coefficients(terms=4):
    f = 0.5 * np.cos(np.pi * (np.arange(400) + 0.5) / 800)
    target = math.sqrt(2.0) * np.sin(np.pi * f)
    basis = np.stack([f ** (2 * k + 1) for k in range(terms)], axis=1)
    return [float(c) for c in np.linalg.lstsq(basis, target, rcond=None)[0]]


SINE = sine_coefficients()


def rounded(v):
    return v.astype(BF).astype(F32)


def split3(v):
    a = rounded(v)
    b = rounded(v - a)
    return a, b, v - a - b


def pick3(rows, x, y, z):
    m = rows % 3
    return jnp.where(m == 0, x, jnp.where(m == 1, y, z))


def dot(a, b):
    return jnp.dot(a, b, preferred_element_type=F32)


def dense_rows(count):
    return (count + 7) & -8


def row_ranges(counts_row):
    leaves = counts_row.shape[1]
    sub = lax.broadcasted_iota(jnp.int32, (leaves, leaves), 0)
    lane = lax.broadcasted_iota(jnp.int32, (leaves, leaves), 1)
    size = jnp.broadcast_to(dense_rows(counts_row), (leaves, leaves)).astype(F32)
    first = jnp.sum(jnp.where(lane < sub, size, 0.0), axis=1, keepdims=True)
    last = jnp.sum(jnp.where(lane <= sub, size, 0.0), axis=1, keepdims=True)
    return first.astype(jnp.int32), last.astype(jnp.int32)


def up_kernel(
    counts_ref, centres_ref, high_ref, stacked_ref, counts_row_ref, freqs_ref, phases_ref, m2m_ref, send_ref,
    basis_ref, nodes_ref, out_ref, sel_ref, dense, total, mult,
):
    leaves = counts_row_ref.shape[1]
    rows = lax.broadcasted_iota(jnp.int32, (32, LEAF), 0)

    def pack(l, off):
        part = [jnp.broadcast_to(stacked_ref[pl.ds(c * leaves + l, 1), :], (32, LEAF)) for c in range(4)]
        rel = pick3(rows, *[part[c] - centres_ref[c * leaves + l] for c in range(3)])
        a, b, c = split3(rel)
        full = jnp.where(
            rows < 9, a,
            jnp.where(rows < 15, b, jnp.where(rows < 18, c, jnp.where(rows < 21, 1.0, jnp.where(rows == 24, part[3], 0.0)))),
        )
        dense[pl.ds(pl.multiple_of(off, 8), LEAF), :] = full.T
        return off + dense_rows(counts_ref[l])

    def pack4(i, off):
        for k in range(4):
            off = pack(i * 4 + k, off)
        return off

    used = lax.fori_loop(0, leaves // 4, pack4, jnp.int32(0))
    dense[pl.ds(pl.multiple_of(used, 8), ROWS), :] = jnp.zeros((ROWS, 32), F32)

    wide_rows = lax.broadcasted_iota(jnp.int32, (32, MP), 0)
    turn = pick3(wide_rows, *[jnp.broadcast_to(freqs_ref[c:c + 1, :], (32, MP)) for c in range(3)])
    turn = jnp.where(wide_rows < 18, turn, jnp.broadcast_to(phases_ref[...], (32, MP))) * (0.5 / math.pi)
    a, b, c = split3(turn)
    g = wide_rows // 3
    weights = jnp.where(
        wide_rows < 18,
        jnp.where((g == 0) | (g == 3) | (g == 5), a, jnp.where((g == 1) | (g == 4), b, c)),
        jnp.where(wide_rows == 18, a, jnp.where(wide_rows == 19, b, jnp.where(wide_rows == 20, c, 0.0))),
    ).astype(BF)

    first, last = row_ranges(counts_row_ref[...])
    lane = lax.broadcasted_iota(jnp.int32, (leaves, ROWS), 1)
    total[...] = jnp.zeros_like(total)

    def step(i, _):
        base = pl.multiple_of(i * ROWS, ROWS)
        rel = dense[pl.ds(base, ROWS), :]
        turns = dot(rel.astype(BF), weights)
        f = turns - jnp.round(turns)
        u = f * f
        s = SINE[3]
        for k in (2, 1, 0):
            s = s * u + SINE[k]
        s = s * f
        basis = 1.0 - s * s
        basis_ref[pl.ds(base, ROWS), :] = basis.astype(BF)
        w = basis * rel[:, 24:25]
        hi = w.astype(BF)
        lo = (w - hi.astype(F32)).astype(BF)
        member = ((lane >= first - base) & (lane < last - base)).astype(F32).astype(BF)
        total[...] += dot(member, hi) + dot(member, lo)
        return 0

    lax.fori_loop(0, (used + ROWS - 1) // ROWS, step, 0)
    leaf_mult = (total[...] * LEAF ** (-0.5)).astype(BF)
    for h in range(2):
        mult[h, :, :] = leaf_mult[:, h * LEAF:(h + 1) * LEAF].astype(F32)
    parents = leaves // 8
    parent = jnp.zeros((parents, MP), F32)
    for c in range(8):
        child = jnp.concatenate([mult[h, pl.ds(c, parents, stride=8), :] for h in range(2)], axis=1)
        parent += dot(child.astype(BF), m2m_ref[c])
    nodes_ref[0:leaves, :] = leaf_mult
    nodes_ref[leaves:leaves + parents, :] = parent.astype(BF)
    ids = lax.broadcasted_iota(jnp.int32, (SHIFTS * CAP, leaves + parents), 1)
    chosen = (send_ref[...] == ids).astype(F32).astype(BF)
    out_ref[...] = dot(chosen, nodes_ref[...]).astype(BF)
    half = REACH * CAP
    sel_ref[...] = out_ref[pl.ds(pl.multiple_of((1 - high_ref[0]) * half, half), half), :]


def slots_kernel(gy_ref, out_ref, recv_ref, slots_ref):
    gy = gy_ref[0]
    for t in range(SHIFTS):
        for sub in range(2):
            ahead = (t - gy) if sub == 0 else (gy - t)
            b = (ahead & (SHIFTS - 1)) - 1
            valid = (b >= 0) & (b < REACH)
            b = jnp.clip(b, 0, REACH - 1)
            own = out_ref[pl.ds(pl.multiple_of((sub * REACH + b) * CAP, CAP), CAP), :]
            far = recv_ref[pl.ds(pl.multiple_of(b * CAP, CAP), CAP), :]
            value = jnp.where(ahead > 0, own, far)
            slots_ref[pl.ds((2 * t + sub) * CAP, CAP), :] = jnp.where(valid, value, jnp.zeros_like(value))


NEAR_BIG, NEAR_SMALL = 64, 32


def near_kernel(
    counts_ref, us_ref, prev_ref, own_ref, next_ref, usv_ref,
    near_ref, feat, charge, tgt, acc_ref, big, small,
):
    leaves = near_ref.shape[0]
    rows = lax.broadcasted_iota(jnp.int32, (8, LEAF), 0)

    def coords(ref, l):
        return [jnp.broadcast_to(ref[pl.ds(c * leaves + l, 1), :] - 2.0, (8, LEAF)) for c in range(3)]

    for part, ref in enumerate((prev_ref, own_ref, next_ref)):

        def build(i, _, part=part, ref=ref):
            for k in range(8):
                l = i * 8 + k
                x, y, z = coords(ref, l)
                n1, n2, n3 = split3(x * x + y * y + z * z)
                s1, s2, s3 = split3(-2.0 * pick3(rows, x, y, z))
                a = jnp.where(rows < 3, s1, jnp.where(rows < 6, s2, jnp.where(rows == 6, n1, n2)))
                b = jnp.where(rows < 3, s3, jnp.where(rows == 3, n3, 1.0))
                s = part * leaves + l
                feat[pl.ds(pl.multiple_of(s * 16, 16), 16), :] = jnp.concatenate([a, b], axis=0).astype(BF)
                charge[pl.ds(pl.multiple_of(s * 8, 8), 8), :] = jnp.broadcast_to(
                    ref[pl.ds(3 * leaves + l, 1), :], (8, LEAF)
                )
            return 0

        lax.fori_loop(0, leaves // 8, build, 0)

    def targets(i, _):
        for k in range(4):
            l = i * 4 + k
            x, y, z = coords(own_ref, l)
            n1, n2, n3 = split3(x * x + y * y + z * z + 0.01)
            s1, s2, s3 = split3(pick3(rows, x, y, z))
            zero = jnp.zeros_like(x)
            a1 = jnp.where(rows < 6, s1, 1.0)
            tail = jnp.where(rows == 5, n1, jnp.where(rows == 6, n2, n3))
            b1 = jnp.where(rows < 3, s1, jnp.where(rows == 3, 1.0, jnp.where(rows == 4, 0.0, tail)))
            a2 = jnp.where(rows < 6, s2, 0.0)
            a3 = jnp.where(rows < 3, s3, 0.0)
            full = jnp.concatenate([a1, b1, a2, zero, a3, zero], axis=0)
            tgt[pl.ds(pl.multiple_of(l * LEAF, LEAF), LEAF), :] = full.T.astype(BF)
        return 0

    lax.fori_loop(0, leaves // 4, targets, 0)

    def listing(l, state):
        n, m = state
        count = counts_ref[l]
        for c in range(LEAF // NEAR_BIG):
            left = count - c * NEAR_BIG
            place = l * LEAF + c * NEAR_BIG
            big[n] = place
            n = n + (left > NEAR_SMALL).astype(jnp.int32)
            small[m] = place
            m = m + ((left > 0) & (left <= NEAR_SMALL)).astype(jnp.int32)
        return n, m

    n_big, n_small = lax.fori_loop(0, leaves, listing, (jnp.int32(0), jnp.int32(0)))

    def run(items, n, size, unroll):
        for k in range(unroll):
            items[n + k] = leaves * LEAF

        def work(i, _):
            for k in range(unroll):
                place = items[i * unroll + k]
                safe = jnp.minimum(place, leaves * LEAF - NEAR_BIG)
                l = safe >> 7
                lhs = tgt[pl.ds(pl.multiple_of(safe, NEAR_SMALL), size), :]
                acc = None
                for u in range(0, ULIST, 2):
                    two = [us_ref[l * ULIST + v] for v in range(u, min(u + 2, ULIST))]
                    f = [feat[pl.ds(pl.multiple_of(s * 16, 16), 16), :] for s in two]
                    f = jnp.concatenate(f, axis=1) if len(f) > 1 else f[0]
                    r = lax.rsqrt(dot(lhs, jnp.concatenate([f, f, f], axis=0)))
                    for j, s in enumerate(two):
                        q = charge[pl.ds(pl.multiple_of(s * 8, 8), 8), :]
                        term = r[:, j * LEAF:(j + 1) * LEAF].reshape(size // 8, 8, LEAF) * q[None]
                        acc = term if acc is None else acc + term
                acc_ref[pl.ds(pl.multiple_of(place, NEAR_SMALL), size), :] = acc.reshape(size, LEAF)
            return 0

        lax.fori_loop(0, (n + unroll - 1) // unroll, work, 0)

    run(big, n_big, NEAR_BIG, 4)
    run(small, n_small, NEAR_SMALL, 4)

    def reduce(i, _):
        parts = []
        for k in range(8):
            l = i * 8 + k
            t = acc_ref[pl.ds(pl.multiple_of(l * LEAF, LEAF), LEAF), :].T
            parts.append(jnp.sum(t, axis=0, keepdims=True))
        near_ref[pl.ds(pl.multiple_of(i * 8, 8), 8), :] = jnp.concatenate(parts, axis=0)
        return 0

    lax.fori_loop(0, leaves // 8, reduce, 0)
    own_id = lax.broadcasted_iota(jnp.int32, usv_ref.shape, 0) + leaves
    times = jnp.sum((usv_ref[...] == own_id).astype(F32), axis=1, keepdims=True)
    itself = own_ref[3 * leaves:4 * leaves, :] * lax.rsqrt(jnp.full((1, LEAF), 0.01, F32))
    near_ref[...] = (near_ref[...] - times * itself) * (ULIST * LEAF) ** (-0.5)


GROUP = 16


def down_kernel(
    counts_ref, gy_ref, counts_row_ref, counts_col_ref, nodes_ref, got_ref, vs_ref, vo_ref, near_ref, m2l_hbm, basis_hbm,
    pot_ref, m2l, basis, table, source, offset, tally, summed, local, far, sems,
):
    leaves = near_ref.shape[0]
    m2l_copy = pltpu.make_async_copy(m2l_hbm, m2l, sems.at[0])
    basis_copy = pltpu.make_async_copy(basis_hbm, basis, sems.at[1])
    m2l_copy.start()
    basis_copy.start()
    gy = gy_ref[0]
    own = nodes_ref.shape[0]
    table[0:own, :] = nodes_ref[...]
    for s in range(SHIFTS):
        by = s + 1 if s < REACH else REACH - 1 - s
        block = 2 * ((gy - by) & (SHIFTS - 1)) + (0 if by > 0 else 1)
        table[own + s * CAP:own + (s + 1) * CAP, :] = got_ref[pl.ds(pl.multiple_of(block * CAP, CAP), CAP), :]
    top = own + SHIFTS * CAP
    table[top:, :] = jnp.zeros((table.shape[0] - top, MP), BF)
    source[...] = jnp.full_like(source, -1)
    source[:, 0:VLIST] = vs_ref[...]
    offset[...] = jnp.full_like(offset, -1)
    offset[:, 0:VLIST] = vo_ref[...]
    sub = lax.broadcasted_iota(jnp.int32, (MP, MP), 0).astype(F32).astype(BF)
    one, zero = jnp.ones((), BF), jnp.zeros((), BF)

    def group(g, _):
        for k in range(GROUP):
            l = g * GROUP + k
            o_row = offset[pl.ds(l, 1), :].astype(F32).astype(BF)
            o_hot = jnp.where(sub[0:OFFSETS] == o_row, one, zero)
            s_row = source[pl.ds(l, 1), :]
            for t in range(3):
                size = min(MP, top - t * MP)
                part = jnp.clip(s_row - t * MP, -1, MP).astype(F32).astype(BF)
                s_hot = jnp.where(sub[0:size] == part, one, zero)
                if size < MP:
                    s_hot = jnp.concatenate([s_hot, jnp.zeros((MP - size, MP), BF)], axis=0)
                tally[k * OFFSETS:(k + 1) * OFFSETS, t * MP:(t + 1) * MP] = lax.dot_general(
                    o_hot, s_hot, NT, preferred_element_type=F32
                ).astype(BF)
        both = dot(tally[...], table[...])
        for h in range(2):
            summed[h, pl.ds(pl.multiple_of(g * GROUP * OFFSETS, GROUP * OFFSETS), GROUP * OFFSETS), :] = both[
                :, h * LEAF:(h + 1) * LEAF
            ]
        return 0

    lax.fori_loop(0, leaves // GROUP, group, 0)
    m2l_copy.wait()
    local[...] = jnp.zeros_like(local)

    def translate(i, _):
        parts = [
            summed[h, pl.ds(i * 4 + k, leaves, stride=OFFSETS), :].astype(BF) for k in range(4) for h in range(2)
        ]
        local[...] += dot(jnp.concatenate(parts, axis=1), m2l[pl.ds(pl.multiple_of(i * 4 * MP, 4 * MP), 4 * MP), :])
        return 0

    lax.fori_loop(0, OFFSETS // 4, translate, 0)
    hi = local[...].astype(BF)
    lo = (local[...] - hi.astype(F32)).astype(BF)
    both = jnp.concatenate([hi, lo], axis=0)
    first, last = row_ranges(counts_row_ref[...])
    used = lax.fori_loop(0, leaves, lambda l, off: off + dense_rows(counts_ref[l]), jnp.int32(0))
    lane = lax.broadcasted_iota(jnp.int32, (leaves, ROWS), 1)
    basis_copy.wait()

    def expand(i, _):
        base = pl.multiple_of(i * ROWS, ROWS)
        p = lax.dot_general(both, basis[pl.ds(base, ROWS), :], NT, preferred_element_type=F32)
        p = p[:leaves] + p[leaves:]
        member = (lane >= first - base) & (lane < last - base)
        value = jnp.sum(jnp.where(member, p, 0.0), axis=0, keepdims=True)
        far[pl.ds(2 * i, 1), :] = value[:, :LEAF]
        far[pl.ds(2 * i + 1, 1), :] = value[:, LEAF:]
        return 0

    lax.fori_loop(0, (used + ROWS - 1) // ROWS, expand, 0)
    lane1 = lax.broadcasted_iota(jnp.int32, (1, LEAF), 1)

    def place(i, off):
        parts = []
        for k in range(8):
            l = i * 8 + k
            row, at = off >> 7, off & (LEAF - 1)
            shift = (LEAF - at) & (LEAF - 1)
            a = pltpu.roll(far[pl.ds(row, 1), :], shift, 1)
            b = pltpu.roll(far[pl.ds(row + 1, 1), :], shift, 1)
            parts.append(jnp.where(lane1 < LEAF - at, a, b))
            off = off + dense_rows(counts_ref[l])
        pot_ref[pl.ds(pl.multiple_of(i * 8, 8), 8), :] = jnp.concatenate(parts, axis=0)
        return off

    lax.fori_loop(0, leaves // 8, place, jnp.int32(0))
    lane = lax.broadcasted_iota(jnp.int32, (leaves, LEAF), 1)
    value = pot_ref[...] * MP ** (-0.5) + near_ref[...]
    pot_ref[...] = jnp.where(lane < counts_col_ref[...], value, 0.0)


def per_device(
    positions, charges, counts, centres, freqs, phases, m2m, m2l, send_nodes, v_source, v_offset, u_source
):
    leaves = counts.shape[0]
    n_gx, n_gy = lax.axis_size("gx"), lax.axis_size("gy")
    devices = n_gx * n_gy
    gy = lax.axis_index("gy").astype(jnp.int32).reshape(1)
    high = (gy >= n_gy // 2).astype(jnp.int32)
    live = jnp.arange(LEAF, dtype=jnp.int32)[None, :] < counts[:, None]
    charge = jnp.where(live, charges.reshape(leaves, LEAF), 0.0)
    stacked = jnp.concatenate([positions.reshape(3 * leaves, LEAF), charge], axis=0)
    up = [(i, i + 1) for i in range(devices - 1)]
    prev = lax.ppermute(stacked, AXES, up)
    after = lax.ppermute(stacked, AXES, [(j, i) for i, j in up])

    counts_row = counts.reshape(1, leaves)
    dense_max = leaves * LEAF + ROWS
    nodes_dev = leaves + leaves // 8
    basis, nodes, outgoing, sel = pl.pallas_call(
        up_kernel,
        out_shape=(
            jax.ShapeDtypeStruct((dense_max, MP), BF),
            jax.ShapeDtypeStruct((nodes_dev, MP), BF),
            jax.ShapeDtypeStruct((SHIFTS * CAP, MP), BF),
            jax.ShapeDtypeStruct((REACH * CAP, MP), BF),
        ),
        in_specs=[SM, SM, SM, VM, VM, VM, VM, VM, VM],
        out_specs=(VM, VM, VM, VM),
        scratch_shapes=[
            pltpu.VMEM((dense_max + LEAF, 32), F32),
            pltpu.VMEM((leaves, MP), F32),
            pltpu.VMEM((2, leaves, LEAF), F32),
        ],
        compiler_params=pltpu.CompilerParams(vmem_limit_bytes=40 * MIB),
        cost_estimate=pl.CostEstimate(flops=10**9, bytes_accessed=10**7, transcendentals=4 * 10**6),
        name="upward",
    )(
        counts, centres.reshape(3 * leaves), high, stacked, counts_row, freqs, phases.reshape(1, MP), m2m,
        send_nodes.reshape(SHIFTS * CAP, 1),
    )

    across = []
    for i in range(devices):
        x, y = i // n_gy, i % n_gy
        to = x + 1 if y >= n_gy // 2 else x - 1
        if 0 <= to < n_gx:
            across.append((i, to * n_gy + y))
    recv = lax.ppermute(sel, AXES, across)
    slots = pl.pallas_call(
        slots_kernel,
        out_shape=jax.ShapeDtypeStruct((2 * SHIFTS * CAP, MP), BF),
        in_specs=[SM, VM, VM],
        out_specs=VM,
        name="slots",
    )(gy, outgoing, recv)
    got = lax.all_to_all(slots.reshape(n_gy, 2 * CAP, MP), "gy", 0, 0).reshape(2 * SHIFTS * CAP, MP)

    near = pl.pallas_call(
        near_kernel,
        out_shape=jax.ShapeDtypeStruct((leaves, LEAF), F32),
        in_specs=[SM, SM, VM, VM, VM, VM],
        out_specs=VM,
        scratch_shapes=[
            pltpu.VMEM((3 * leaves * 16, LEAF), BF),
            pltpu.VMEM((3 * leaves * 8, LEAF), F32),
            pltpu.VMEM((leaves * LEAF, 48), BF),
            pltpu.VMEM((leaves * LEAF + NEAR_BIG, LEAF), F32),
            pltpu.SMEM((2 * leaves + 16,), jnp.int32),
            pltpu.SMEM((2 * leaves + 16,), jnp.int32),
        ],
        compiler_params=pltpu.CompilerParams(vmem_limit_bytes=40 * MIB),
        cost_estimate=pl.CostEstimate(flops=5 * 10**9, bytes_accessed=10**6, transcendentals=4 * 10**7),
        name="near",
    )(counts, u_source.reshape(leaves * ULIST), prev, stacked, after, u_source)

    table_rows = 3 * MP
    out = pl.pallas_call(
        down_kernel,
        out_shape=jax.ShapeDtypeStruct((leaves, LEAF), F32),
        in_specs=[SM, SM, VM, VM, VM, VM, VM, VM, VM, HBM, HBM],
        out_specs=VM,
        scratch_shapes=[
            pltpu.VMEM((OFFSETS * MP, MP), BF),
            pltpu.VMEM((dense_max, MP), BF),
            pltpu.VMEM((table_rows, MP), BF),
            pltpu.VMEM((leaves, MP), jnp.int32),
            pltpu.VMEM((leaves, MP), jnp.int32),
            pltpu.VMEM((GROUP * OFFSETS, table_rows), BF),
            pltpu.VMEM((2, leaves * OFFSETS, LEAF), F32),
            pltpu.VMEM((leaves, MP), F32),
            pltpu.VMEM((dense_max // LEAF + 2, LEAF), F32),
            pltpu.SemaphoreType.DMA((2,)),
        ],
        compiler_params=pltpu.CompilerParams(vmem_limit_bytes=56 * MIB),
        cost_estimate=pl.CostEstimate(flops=2 * 10**10, bytes_accessed=2 * 10**7, transcendentals=0),
        name="downward",
    )(
        counts, gy, counts_row, counts.reshape(leaves, 1), nodes, got, v_source, v_offset, near,
        m2l.reshape(OFFSETS * MP, MP), basis,
    )
    return out.reshape(leaves * LEAF)


def solution(mesh):
    both = P(AXES)
    cols = P(None, AXES)
    in_specs = (
        cols, both, both, cols, P(), P(), P(), P(), P(AXES, None, None), P(AXES, None), P(AXES, None), P(AXES, None),
    )
    return jax.shard_map(per_device, mesh=mesh, in_specs=in_specs, out_specs=both, check_vma=False)
```

time: 762 us -> 142 us (0.19); the launches traced: 750 us -> 139 us
  other arithmetic: 391 us -> 0.94 us
  matrix products: 173 us -> 0 us
  Pallas kernels: 0 us -> 99.9 us
  local copies, waits for them, and re-layouts: 113 us -> 15.4 us
  starting transfers between devices: 67.4 us -> 20.5 us
    reduce_sum x32 -> x0, other arithmetic: 385 us -> none  [the longest x16 269 us: group_fn(): dist2 = jnp.sum(diff * diff, axis=0)]
    dot_general x6 -> x0, matrix products: 173 us -> none  [the longest x1 70.5 us: per_device(): jnp.einsum('ln,lnk->lk', charge, basis, precision=lax.Precision.HIGHEST)]
    gather x19 -> x0, local copies, waits for them, and re-layouts: 101 us -> none  [the longest x2 83.8 us: per_device(): gathered = table[v_source]]
    pallas_call x0 -> x4, Pallas kernels: none -> 99.9 us  [the longest x1 39.3 us: per_device(): pl.pallas_call(near_kernel, out_shape=jax.ShapeDtypeStruct((leaves, LEAF)...]
    ppermute x18 -> x3, starting transfers between devices: 67.4 us -> 9.75 us  [the longest x1 5.92 us: per_device(): after = lax.ppermute(stacked, AXES, [(j, i) for i, j in up])]
    all_to_all x0 -> x1, starting transfers between devices: none -> 10.7 us  [per_device(): lax.all_to_all(slots.reshape(n_gy, 2 * CAP, MP), 'gy', 0, 0)]
  transfers between devices with their start and end apart: 18 -> 4, of which waited for: 1 -> 1; matrix products, arithmetic and copies ran while one was open for 35% -> 3% of each run, Pallas kernels for 0% -> 45%
where the time goes in v1:
time: 142 us; the launch traced here: 139 us
  Pallas kernels  99.9 us (70%)
  starting transfers between devices  20.5 us (14%)
  local copies, waits for them, and re-layouts  15.4 us (11%)
  waiting for transfers between devices  2.51 us (2%)
    pallas_call x1, Pallas kernels, per_device(): pl.pallas_call(near_kernel, out_shape=jax.ShapeDtypeStruct((leaves, LEAF)...  39.3 us
    pallas_call x1, Pallas kernels, per_device(): pl.pallas_call(down_kernel, out_shape=jax.ShapeDtypeStruct((leaves, LEAF)...  36.7 us
    pallas_call x1, Pallas kernels, per_device(): pl.pallas_call(up_kernel, out_shape=(jax.ShapeDtypeStruct((dense_max, MP)...  21.8 us
    unnamed x33, local copies, waits for them, and re-layouts  12.4 us
    all_to_all x1, starting transfers between devices, per_device(): lax.all_to_all(slots.reshape(n_gy, 2 * CAP, MP), 'gy', 0, 0)  10.7 us
    ppermute x1, starting transfers between devices, per_device(): after = lax.ppermute(stacked, AXES, [(j, i) for i, j in up])  5.92 us
  transfers between devices with their start and end apart: 4, of which 1 were waited for; matrix products, arithmetic and copies ran while one was open for 3% of the time, Pallas kernels for 45%

profile of v1, /device:TPU:10, one launch (start us, length us, event | category | flops | bytes accessed | tf_op | source)
XLA Modules:
  0.0 139.4 jit_solution(2609206195232921615)
XLA Ops:
  0.0 1.1 reshape.44
  1.2 0.9 bitcast_select_fusion
  2.1 5.9 %collective-permute-start.2 = (f32[512,128]{1,0:T(8,128)S(1)}, f32[512,128]{1,0:T(8,128)S(1)}, u32[]{:S(2)}, u32[]{:S(2)}) collective-permute-start(f32[512,128]{1,0:T(8,128)S(1)} %pad_maximum_fusion.stacked_ref.own_ref), channel_id=1, source_target_pairs={{1,0},{2,1},{3,2},{4,3},{5,4},{6,5},{7,6},{8,7},{9,8},{10,9},{11,1... | collective-permute-start | bytes 786440 | tf_op jit(solution)/shard_map/ppermute | solution.py:388
  8.0 1.9 %collective-permute-start.1 = (f32[512,128]{1,0:T(8,128)S(1)}, f32[512,128]{1,0:T(8,128)S(1)}, u32[]{:S(2)}, u32[]{:S(2)}) collective-permute-start(f32[512,128]{1,0:T(8,128)S(1)} %pad_maximum_fusion.stacked_ref.own_ref), channel_id=1, source_target_pairs={{0,1},{1,2},{2,3},{3,4},{4,5},{5,6},{6,7},{7,8},{8,9},{9,10},{10,1... | collective-permute-start | bytes 786440 | tf_op jit(solution)/shard_map/ppermute | solution.py:387
  10.0 1.0 reshape.53.send_ref
  10.9 0.0 copy-start.1
  11.0 0.6 copy-done.1
  11.6 1.2 copy-done.3
  12.8 0.7 copy-done.4
  13.5 0.7 copy-done.5
  14.2 0.7 copy-done.6
  14.9 21.8 %upward.1 = (bf16[16640,256]{1,0:T(8,128)(2,1)S(1)}, bf16[144,256]{1,0:T(8,128)(2,1)S(1)}, bf16[512,256]{1,0:T(8,128)(2,1)S(1)}, bf16[256,256]{1,0:T(8,128)(2,1)S(1)}) custom-call(s32[128]{0:T(128)S(1)} %copy-done.1, f32[384]{0:T(512)S(1)} %bitcast.14, s32[1]{0:T(128)S(6)} %convert_element_type.3.high_ref, ...), custom_call_target="tpu_custom_call" | custom-call | flops 1000000000 | bytes 10000000 | tf_op jit(solution)/shard_map/upward/pallas_call | solution.py:393
  36.7 0.7 copy-done
  37.4 3.3 %copy-done.7 = bf16[16640,256]{1,0:T(8,128)(2,1)} copy-done((bf16[16640,256]{1,0:T(8,128)(2,1)}, bf16[16640,256]{1,0:T(8,128)(2,1)S(1)}, u32[]{:S(2)}) %copy-start.7) | copy-done | bytes 8519704
  40.8 0.6 copy-done.8
  41.4 1.9 %collective-permute-start = (bf16[256,256]{1,0:T(8,128)(2,1)S(1)}, bf16[256,256]{1,0:T(8,128)(2,1)S(1)}, u32[]{:S(2)}, u32[]{:S(2)}) collective-permute-start(bf16[256,256]{1,0:T(8,128)(2,1)S(1)} %get-tuple-element.11), channel_id=1, source_target_pairs={{8,24},{9,25},{10,26},{11,27},{12,28},{13,29},{14,30},{15,31},{16,... | collective-permute-start | bytes 393224 | tf_op jit(solution)/shard_map/ppermute | solution.py:422
  43.3 2.5 %collective-permute-done.recv_ref = bf16[256,256]{1,0:T(8,128)(2,1)S(1)} collective-permute-done((bf16[256,256]{1,0:T(8,128)(2,1)S(1)}, bf16[256,256]{1,0:T(8,128)(2,1)S(1)}, u32[]{:S(2)}, u32[]{:S(2)}) %collective-permute-start) | collective-permute-done | bytes 131104 | tf_op jit(solution)/shard_map/ppermute | solution.py:422
  45.8 0.7 copy-done.11
  46.5 2.0 %slots.1 = bf16[1024,256]{1,0:T(8,128)(2,1)} custom-call(s32[1]{0:T(128)} %bitcast.gy_ref, bf16[512,256]{1,0:T(8,128)(2,1)} %copy-done, bf16[256,256]{1,0:T(8,128)(2,1)} %copy-done.11), custom_call_target="tpu_custom_call" | custom-call | tf_op jit(solution)/shard_map/slots/pallas_call | solution.py:423
  48.5 10.7 %all-to-all-start = ((bf16[16,64,256]{2,1,0:T(8,128)(2,1)}), bf16[16,64,256]{2,1,0:T(8,128)(2,1)S(1)}, u32[]{:S(2)}, u32[]{:S(2)}) async-start(bf16[16,64,256]{2,1,0:T(8,128)(2,1)} %bitcast.16), calls=%async_computation | async-start | bytes 1048576 | tf_op jit(solution)/shard_map/all_to_all | solution.py:430
  59.2 0.1 copy.18.usv_ref
  59.3 0.2 reshape.50.us_ref
  59.5 0.7 copy.20.counts_col_ref
  60.3 0.7 copy.21.vs_ref
  61.0 0.8 copy.22.vo_ref
  61.8 0.0 collective-permute-done.2.next_ref
  61.8 0.0 collective-permute-done.1.prev_ref
  61.8 39.3 %near.1.near_ref = f32[128,128]{1,0:T(8,128)S(1)} custom-call(s32[128]{0:T(128)S(1)} %copy-done.2, s32[3456]{0:T(1024)S(1)} %reshape.50.us_ref, f32[512,128]{1,0:T(8,128)S(1)} %collective-permute-done.1.prev_ref, f32[512,128]{1,0:T(8,128)S(1)} %pad_maximum_fusion.stacked_ref.own_ref, f32[512,128]{1,0:T(8,128)S(1)} %collective-permute-done.2.next_ref, ...), custom_call_target="tpu_custom_call" | custom-call | flops 5000000000 | bytes 1000000 | tf_op jit(solution)/shard_map/near/pallas_call | solution.py:432
  101.1 0.6 copy-done.9
  101.8 0.0 all-to-all-done
  101.8 0.9 copy-done.10
  102.6 36.7 %downward.1 = f32[128,128]{1,0:T(8,128)} custom-call(s32[128]{0:T(128)} %counts_ref.5, s32[1]{0:T(128)} %bitcast.gy_ref, s32[1,128]{1,0:T(1,128)} %bitcast.11, s32[128,1]{1,0:T(8,128)} %copy.20.counts_col_ref, bf16[144,256]{1,0:T(8,128)(2,1)} %copy-done.8, bf16[1024,256]{1,0:T(8,128)(2,1)} %bitcast.17, s32[128,189]{1,0:T(8,128)} %copy.21.vs_ref, ...), custom_call_target="tpu_custom_call" | custom-call | flops 20000000000 | bytes 20000000 | tf_op jit(solution)/shard_map/downward/pallas_call | solution.py:451
  (19 shorter events, 0.1 us)
Async XLA Ops:
  0.0 59.5 %copy-start.2 = (s32[128]{0:T(128)S(1)}, s32[128]{0:T(128)}, u32[]{:S(2)}) copy-start(s32[128]{0:T(128)} %counts_ref.5) | copy-start | bytes 1540
  0.0 59.2 %copy-start.14 = (s32[128,27]{0,1:T(8,128)S(1)}, s32[128,27]{0,1:T(8,128)}, u32[]{:S(2)}) copy-start(s32[128,27]{0,1:T(8,128)} %param.23) | copy-start | bytes 41476
  0.0 60.3 %copy-start.12 = (s32[128,189]{0,1:T(8,128)S(1)}, s32[128,189]{0,1:T(8,128)}, u32[]{:S(2)}) copy-start(s32[128,189]{0,1:T(8,128)} %param.21) | copy-start | bytes 290308
  0.0 61.0 %copy-start.13 = (s32[128,189]{0,1:T(8,128)S(1)}, s32[128,189]{0,1:T(8,128)}, u32[]{:S(2)}) copy-start(s32[128,189]{0,1:T(8,128)} %param.22) | copy-start | bytes 290308
  2.1 59.7 %collective-permute-start.2 = (f32[512,128]{1,0:T(8,128)S(1)}, f32[512,128]{1,0:T(8,128)S(1)}, u32[]{:S(2)}, u32[]{:S(2)}) collective-permute-start(f32[512,128]{1,0:T(8,128)S(1)} %pad_maximum_fusion.stacked_ref.own_ref), channel_id=1, source_target_pairs={{1,0},{2,1},{3,2},{4,3},{5,4},{6,5},{7,6},{8,7},{9,8},{10,9},{11,1... | collective-permute-start | bytes 786440 | tf_op jit(solution)/shard_map/ppermute | solution.py:388
  8.0 53.7 %collective-permute-start.1 = (f32[512,128]{1,0:T(8,128)S(1)}, f32[512,128]{1,0:T(8,128)S(1)}, u32[]{:S(2)}, u32[]{:S(2)}) collective-permute-start(f32[512,128]{1,0:T(8,128)S(1)} %pad_maximum_fusion.stacked_ref.own_ref), channel_id=1, source_target_pairs={{0,1},{1,2},{2,3},{3,4},{4,5},{5,6},{6,7},{7,8},{8,9},{9,10},{10,1... | collective-permute-start | bytes 786440 | tf_op jit(solution)/shard_map/ppermute | solution.py:387
  10.9 0.7 copy-start.1
  11.6 1.2 copy-start.3
  12.8 0.7 copy-start.4
  13.5 0.7 copy-start.5
  14.2 0.7 copy-start.6
  36.7 0.7 copy-start
  37.4 3.3 %copy-start.7 = (bf16[16640,256]{1,0:T(8,128)(2,1)}, bf16[16640,256]{1,0:T(8,128)(2,1)S(1)}, u32[]{:S(2)}) copy-start(bf16[16640,256]{1,0:T(8,128)(2,1)S(1)} %get-tuple-element.12.basis_hbm) | copy-start | bytes 25559044
  40.8 0.6 copy-start.8
  41.4 4.4 %collective-permute-start = (bf16[256,256]{1,0:T(8,128)(2,1)S(1)}, bf16[256,256]{1,0:T(8,128)(2,1)S(1)}, u32[]{:S(2)}, u32[]{:S(2)}) collective-permute-start(bf16[256,256]{1,0:T(8,128)(2,1)S(1)} %get-tuple-element.11), channel_id=1, source_target_pairs={{8,24},{9,25},{10,26},{11,27},{12,28},{13,29},{14,30},{15,31},{16,... | collective-permute-start | bytes 393224 | tf_op jit(solution)/shard_map/ppermute | solution.py:422
  45.8 0.7 copy-start.11
  48.5 53.3 %all-to-all-start = ((bf16[16,64,256]{2,1,0:T(8,128)(2,1)}), bf16[16,64,256]{2,1,0:T(8,128)(2,1)S(1)}, u32[]{:S(2)}, u32[]{:S(2)}) async-start(bf16[16,64,256]{2,1,0:T(8,128)(2,1)} %bitcast.16), calls=%async_computation | async-start | bytes 1048576 | tf_op jit(solution)/shard_map/all_to_all | solution.py:430
  101.1 0.6 copy-start.9
  101.8 0.9 copy-start.10

commit v2 on v1

v2 whole, which is shorter than its diff:
```python
import functools
import math

import jax
import jax.numpy as jnp
import numpy as np
from jax import lax
from jax.experimental import pallas as pl
from jax.experimental.pallas import tpu as pltpu
from jax.sharding import PartitionSpec as P

F32 = jnp.float32
BF = jnp.bfloat16
MP = 256
LEAF = 128
OFFSETS = 64
VLIST = 189
VPAD = 192
ULIST = 27
CAP = 32
REACH = 8
SHIFTS = 16
AXES = ("gx", "gy")
ROWS = 256
STEP = 512
MIB = 2**20
SM = pl.BlockSpec(memory_space=pltpu.SMEM)
HBM = pl.BlockSpec(memory_space=pl.ANY)


def block(value):
    return pl.BlockSpec(value.shape, lambda i: (0,) * len(value.shape))


NT = (((1,), (1,)), ((), ()))


def sine_coefficients(terms=4):
    f = 0.5 * np.cos(np.pi * (np.arange(400) + 0.5) / 800)
    target = math.sqrt(2.0) * np.sin(np.pi * f)
    basis = np.stack([f ** (2 * k + 1) for k in range(terms)], axis=1)
    return [float(c) for c in np.linalg.lstsq(basis, target, rcond=None)[0]]


SINE = sine_coefficients()


def rounded(v):
    return v.astype(BF).astype(F32)


def split3(v):
    a = rounded(v)
    b = rounded(v - a)
    return a, b, v - a - b


def pick3(rows, x, y, z):
    m = rows % 3
    return jnp.where(m == 0, x, jnp.where(m == 1, y, z))


def dot(a, b):
    return jnp.dot(a, b, preferred_element_type=F32)


def dense_rows(count):
    return (count + 7) & -8


def column(row):
    leaves = row.shape[1]
    sub = lax.broadcasted_iota(jnp.int32, (leaves, leaves), 0)
    lane = lax.broadcasted_iota(jnp.int32, (leaves, leaves), 1)
    return jnp.sum(jnp.where(lane == sub, row.astype(F32), 0.0), axis=1, keepdims=True).astype(jnp.int32)


def row_ranges(counts_row):
    leaves = counts_row.shape[1]
    sub = lax.broadcasted_iota(jnp.int32, (leaves, leaves), 0)
    lane = lax.broadcasted_iota(jnp.int32, (leaves, leaves), 1)
    size = jnp.broadcast_to(dense_rows(counts_row), (leaves, leaves)).astype(F32)
    first = jnp.sum(jnp.where(lane < sub, size, 0.0), axis=1, keepdims=True)
    last = jnp.sum(jnp.where(lane <= sub, size, 0.0), axis=1, keepdims=True)
    return first.astype(jnp.int32), last.astype(jnp.int32)


def up_kernel(
    counts_ref, centres_ref, gy_ref, stacked_ref, counts_row_ref, freqs_ref, phases_ref, send_ref, m2m_hbm,
    basis_hbm, nodes_ref, slots_ref, sel_ref, dense, total, mult, basis, m2m, chosen_rows, sems,
):
    leaves = counts_row_ref.shape[1]
    m2m_copy = pltpu.make_async_copy(m2m_hbm, m2m, sems.at[2])
    m2m_copy.start()
    rows = lax.broadcasted_iota(jnp.int32, (32, LEAF), 0)

    def pack(l, off):
        part = [jnp.broadcast_to(stacked_ref[pl.ds(c * leaves + l, 1), :], (32, LEAF)) for c in range(4)]
        rel = pick3(rows, *[part[c] - centres_ref[c * leaves + l] for c in range(3)])
        a, b, c = split3(rel)
        full = jnp.where(
            rows < 9, a,
            jnp.where(rows < 15, b, jnp.where(rows < 18, c, jnp.where(rows < 21, 1.0, jnp.where(rows == 24, part[3], 0.0)))),
        )
        dense[pl.ds(pl.multiple_of(off, 8), LEAF), :] = full.T
        return off + dense_rows(counts_ref[l])

    def pack8(i, off):
        for k in range(8):
            off = pack(i * 8 + k, off)
        return off

    used = lax.fori_loop(0, leaves // 8, pack8, jnp.int32(0))
    dense[pl.ds(pl.multiple_of(used, 8), STEP), :] = jnp.zeros((STEP, 32), F32)

    wide_rows = lax.broadcasted_iota(jnp.int32, (32, MP), 0)
    turn = pick3(wide_rows, *[jnp.broadcast_to(freqs_ref[c:c + 1, :], (32, MP)) for c in range(3)])
    turn = jnp.where(wide_rows < 18, turn, jnp.broadcast_to(phases_ref[...], (32, MP))) * (0.5 / math.pi)
    a, b, c = split3(turn)
    g = wide_rows // 3
    weights = jnp.where(
        wide_rows < 18,
        jnp.where((g == 0) | (g == 3) | (g == 5), a, jnp.where((g == 1) | (g == 4), b, c)),
        jnp.where(wide_rows == 18, a, jnp.where(wide_rows == 19, b, jnp.where(wide_rows == 20, c, 0.0))),
    ).astype(BF)

    first, last = row_ranges(counts_row_ref[...])
    lane = lax.broadcasted_iota(jnp.int32, (leaves, ROWS), 1)
    total[...] = jnp.zeros_like(total)

    def written(i, slot):
        place = pl.ds(pl.multiple_of(i * STEP, STEP), STEP)
        return pltpu.make_async_copy(basis.at[slot], basis_hbm.at[place, :], sems.at[slot])

    def step(i, _):
        slot = lax.rem(i, 2)

        @pl.when(i >= 2)
        def _():
            written(i - 2, slot).wait()

        sums = []
        for part in range(STEP // ROWS):
            base = pl.multiple_of(i * STEP + part * ROWS, ROWS)
            rel = dense[pl.ds(base, ROWS), :]
            turns = dot(rel.astype(BF), weights)
            f = turns - jnp.round(turns)
            u = f * f
            s = SINE[3]
            for k in (2, 1, 0):
                s = s * u + SINE[k]
            s = s * f
            value = 1.0 - s * s
            basis[slot, part * ROWS:(part + 1) * ROWS, :] = value.astype(BF)
            w = value * rel[:, 24:25]
            hi = w.astype(BF)
            lo = (w - hi.astype(F32)).astype(BF)
            member = ((lane >= first - base) & (lane < last - base)).astype(F32).astype(BF)
            sums.append(dot(member, hi) + dot(member, lo))
        total[...] += sums[0] + sums[1]
        written(i, slot).start()
        return 0

    steps = (used + STEP - 1) // STEP
    lax.fori_loop(0, steps, step, 0)
    leaf_mult = (total[...] * LEAF ** (-0.5)).astype(BF)
    for h in range(2):
        mult[h, :, :] = leaf_mult[:, h * LEAF:(h + 1) * LEAF].astype(F32)
    parents = leaves // 8
    parent = jnp.zeros((parents, MP), F32)
    m2m_copy.wait()
    for c in range(8):
        child = jnp.concatenate([mult[h, pl.ds(c, parents, stride=8), :] for h in range(2)], axis=1)
        parent += dot(child.astype(BF), m2m[c])
    nodes_ref[0:leaves, :] = leaf_mult
    nodes_ref[leaves:leaves + parents, :] = parent.astype(BF)
    ids = lax.broadcasted_iota(jnp.int32, (CAP, leaves + parents), 1).astype(F32)
    wanted = send_ref[...].astype(F32).T
    chosen = jnp.concatenate([(wanted[:, s:s + 1] == ids).astype(F32) for s in range(SHIFTS)], axis=0).astype(BF)
    chosen_rows[...] = dot(chosen, nodes_ref[...]).astype(BF)

    gy = gy_ref[0]
    high = gy >= SHIFTS // 2

    def rows_of(b):
        return chosen_rows[pl.ds(pl.multiple_of(b * CAP, CAP), CAP), :]

    for t in range(SHIFTS):
        for sub in range(2):
            b = ((t - gy) if sub == 0 else (gy - t)) - 1
            valid = (b >= 0) & (b < REACH)
            value = rows_of(sub * REACH + jnp.clip(b, 0, REACH - 1))
            slots_ref[pl.ds((2 * t + sub) * CAP, CAP), :] = jnp.where(valid, value, jnp.zeros_like(value))
    for t in range(SHIFTS // 2):
        b = jnp.where(high, t - gy + SHIFTS - 1, gy - t + SHIFTS // 2 - 1)
        value = rows_of(jnp.where(high, 0, REACH) + jnp.clip(b, 0, REACH - 1))
        sel_ref[pl.ds(t * CAP, CAP), :] = jnp.where(b < REACH, value, jnp.zeros_like(value))
    if_two = steps >= 2

    @pl.when(if_two)
    def _():
        written(steps - 2, lax.rem(steps - 2, 2)).wait()

    written(steps - 1, lax.rem(steps - 1, 2)).wait()


NEAR_BIG, NEAR_SMALL = 64, 32


def near_kernel(
    begin, end, counts_ref, us_ref, prev_ref, own_ref, next_ref, usv_ref,
    near_ref, feat, charge, tgt, acc_ref, big, small,
):
    leaves = own_ref.shape[0] // 4
    rows = lax.broadcasted_iota(jnp.int32, (8, LEAF), 0)

    def coords(ref, l):
        return [jnp.broadcast_to(ref[pl.ds(c * leaves + l, 1), :] - 2.0, (8, LEAF)) for c in range(3)]

    for part, ref in enumerate((prev_ref, own_ref, next_ref)):

        def build(i, _, part=part, ref=ref):
            for k in range(8):
                l = i * 8 + k
                x, y, z = coords(ref, l)
                n1, n2, n3 = split3(x * x + y * y + z * z)
                s1, s2, s3 = split3(-2.0 * pick3(rows, x, y, z))
                a = jnp.where(rows < 3, s1, jnp.where(rows < 6, s2, jnp.where(rows == 6, n1, n2)))
                b = jnp.where(rows < 3, s3, jnp.where(rows == 3, n3, 1.0))
                s = part * leaves + l
                feat[pl.ds(pl.multiple_of(s * 16, 16), 16), :] = jnp.concatenate([a, b], axis=0).astype(BF)
                charge[pl.ds(pl.multiple_of(s * 8, 8), 8), :] = jnp.broadcast_to(
                    ref[pl.ds(3 * leaves + l, 1), :], (8, LEAF)
                )
            return 0

        lax.fori_loop(0, leaves // 8, build, 0)

    def targets(i, _):
        for k in range(8):
            l = i * 8 + k
            x, y, z = coords(own_ref, l)
            n1, n2, n3 = split3(x * x + y * y + z * z + 0.01)
            s1, s2, s3 = split3(pick3(rows, x, y, z))
            zero = jnp.zeros_like(x)
            a1 = jnp.where(rows < 6, s1, 1.0)
            tail = jnp.where(rows == 5, n1, jnp.where(rows == 6, n2, n3))
            b1 = jnp.where(rows < 3, s1, jnp.where(rows == 3, 1.0, jnp.where(rows == 4, 0.0, tail)))
            a2 = jnp.where(rows < 6, s2, 0.0)
            a3 = jnp.where(rows < 3, s3, 0.0)
            full = jnp.concatenate([a1, b1, a2, zero, a3, zero], axis=0)
            tgt[pl.ds(pl.multiple_of(l * LEAF, LEAF), LEAF), :] = full.T.astype(BF)
        return 0

    lax.fori_loop(begin // 8, end // 8, targets, 0)

    def listing(l, state):
        n, m = state
        count = counts_ref[l]
        for c in range(LEAF // NEAR_BIG):
            left = count - c * NEAR_BIG
            place = l * LEAF + c * NEAR_BIG
            big[n] = place
            n = n + (left > NEAR_SMALL).astype(jnp.int32)
            small[m] = place
            m = m + ((left > 0) & (left <= NEAR_SMALL)).astype(jnp.int32)
        return n, m

    n_big, n_small = lax.fori_loop(begin, end, listing, (jnp.int32(0), jnp.int32(0)))

    def run(items, n, size, unroll):
        for k in range(unroll):
            items[n + k] = leaves * LEAF

        def work(i, _):
            for k in range(unroll):
                place = items[i * unroll + k]
                safe = jnp.minimum(place, leaves * LEAF - NEAR_BIG)
                l = safe >> 7
                lhs = tgt[pl.ds(pl.multiple_of(safe, NEAR_SMALL), size), :]
                acc = None
                for u in range(0, ULIST, 2):
                    two = [us_ref[v * leaves + l] for v in range(u, min(u + 2, ULIST))]
                    f = [feat[pl.ds(pl.multiple_of(s * 16, 16), 16), :] for s in two]
                    f = jnp.concatenate(f, axis=1) if len(f) > 1 else f[0]
                    r = lax.rsqrt(dot(lhs, jnp.concatenate([f, f, f], axis=0)))
                    for j, s in enumerate(two):
                        q = charge[pl.ds(pl.multiple_of(s * 8, 8), 8), :]
                        term = r[:, j * LEAF:(j + 1) * LEAF].reshape(size // 8, 8, LEAF) * q[None]
                        acc = term if acc is None else acc + term
                acc_ref[pl.ds(pl.multiple_of(place, NEAR_SMALL), size), :] = acc.reshape(size, LEAF)
            return 0

        lax.fori_loop(0, (n + unroll - 1) // unroll, work, 0)

    run(big, n_big, NEAR_BIG, 8)
    run(small, n_small, NEAR_SMALL, 8)

    def reduce(i, _):
        parts = []
        for k in range(8):
            l = i * 8 + k
            t = acc_ref[pl.ds(pl.multiple_of(l * LEAF, LEAF), LEAF), :].T
            parts.append(jnp.sum(t, axis=0, keepdims=True))
        near_ref[pl.ds(pl.multiple_of(i * 8 - begin, 8), 8), :] = jnp.concatenate(parts, axis=0)
        return 0

    lax.fori_loop(begin // 8, end // 8, reduce, 0)
    own_id = lax.broadcasted_iota(jnp.int32, usv_ref.shape, 1) + leaves
    times = column(jnp.sum((usv_ref[...] == own_id).astype(F32), axis=0, keepdims=True)).astype(F32)
    itself = own_ref[3 * leaves + begin:3 * leaves + end, :] * lax.rsqrt(jnp.full((1, LEAF), 0.01, F32))
    near_ref[...] = (near_ref[...] - times[begin:end] * itself) * (ULIST * LEAF) ** (-0.5)


GROUP = 16
SPREAD = 4


def down_kernel(
    counts_ref, gy_ref, counts_row_ref, nodes_ref, got_ref, vs_ref, vo_ref, near_ref, m2l_hbm, basis_hbm,
    pot_ref, m2l, basis, table, source, offset, tally, summed, local, far, sems,
):
    leaves = counts_row_ref.shape[1]
    m2l_copy = pltpu.make_async_copy(m2l_hbm, m2l, sems.at[0])
    basis_copy = pltpu.make_async_copy(basis_hbm, basis, sems.at[1])
    m2l_copy.start()
    basis_copy.start()
    gy = gy_ref[0]
    own = nodes_ref.shape[0]
    table[0:own, :] = nodes_ref[...]
    for s in range(SHIFTS):
        by = s + 1 if s < REACH else REACH - 1 - s
        block = 2 * ((gy - by) & (SHIFTS - 1)) + (0 if by > 0 else 1)
        table[own + s * CAP:own + (s + 1) * CAP, :] = got_ref[pl.ds(pl.multiple_of(block * CAP, CAP), CAP), :]
    top = own + SHIFTS * CAP
    table[top:, :] = jnp.zeros((table.shape[0] - top, MP), BF)
    offset[...] = jnp.full_like(offset, -1)
    offset[:, 0:VLIST] = vo_ref[...].astype(F32).T
    tally[...] = jnp.zeros_like(tally)
    source[...] = jnp.full_like(source, -1)
    source[:, 0:VLIST] = vs_ref[...].astype(F32).T
    sub = lax.broadcasted_iota(jnp.int32, (MP, MP), 0).astype(F32).astype(BF)
    one, zero = jnp.ones((), BF), jnp.zeros((), BF)
    F8 = jnp.float8_e4m3fn

    def group(g, _):
        for k in range(GROUP):
            l = g * GROUP + k
            o_row = offset[pl.ds(l, 1), :].astype(BF)
            o_hot = jnp.where(sub[0:OFFSETS] == o_row, one, zero).astype(F8)
            s_row = source[pl.ds(l, 1), :]
            for t in range(3):
                size = MP if t < 2 else 160
                part = jnp.clip(s_row - t * MP, -1.0, MP + 0.0).astype(BF)
                s_hot = jnp.where(sub[0:size] == part, one, zero).astype(F8)
                tally[k * OFFSETS:(k + 1) * OFFSETS, t * MP:t * MP + size] = lax.dot_general(
                    o_hot, s_hot, NT, preferred_element_type=F32
                ).astype(BF)
        both = dot(tally[...], table[...]).reshape(GROUP, OFFSETS, MP)
        summed[:, pl.ds(pl.multiple_of(g * GROUP, GROUP), GROUP), :] = jnp.swapaxes(both, 0, 1).astype(BF)
        return 0

    lax.fori_loop(0, leaves // GROUP, group, 0)
    m2l_copy.wait()
    local[...] = jnp.zeros_like(local)

    def translate(i, _):
        parts = [summed[i * 8 + k] for k in range(8)]
        local[...] += dot(jnp.concatenate(parts, axis=1), m2l[pl.ds(pl.multiple_of(i * 8 * MP, 8 * MP), 8 * MP), :])
        return 0

    lax.fori_loop(0, OFFSETS // 8, translate, 0)
    hi = local[...].astype(BF)
    lo = (local[...] - hi.astype(F32)).astype(BF)
    both = jnp.concatenate([hi, lo], axis=0)
    first, last = row_ranges(counts_row_ref[...])
    used = lax.fori_loop(0, leaves, lambda l, off: off + dense_rows(counts_ref[l]), jnp.int32(0))
    lane = lax.broadcasted_iota(jnp.int32, (leaves, ROWS), 1)
    basis_copy.wait()

    def expand(i, _):
        for part in range(SPREAD):
            j = i * SPREAD + part
            base = pl.multiple_of(j * ROWS, ROWS)
            p = lax.dot_general(both, basis[pl.ds(base, ROWS), :], NT, preferred_element_type=F32)
            p = p[:leaves] + p[leaves:]
            member = (lane >= first - base) & (lane < last - base)
            value = jnp.sum(jnp.where(member, p, 0.0), axis=0, keepdims=True)
            far[pl.ds(2 * j, 1), :] = value[:, :LEAF]
            far[pl.ds(2 * j + 1, 1), :] = value[:, LEAF:]
        return 0

    lax.fori_loop(0, (used + SPREAD * ROWS - 1) // (SPREAD * ROWS), expand, 0)
    lane1 = lax.broadcasted_iota(jnp.int32, (1, LEAF), 1)

    def place(i, off):
        parts = []
        for k in range(8):
            l = i * 8 + k
            row, at = off >> 7, off & (LEAF - 1)
            shift = (LEAF - at) & (LEAF - 1)
            a = pltpu.roll(far[pl.ds(row, 1), :], shift, 1)
            b = pltpu.roll(far[pl.ds(row + 1, 1), :], shift, 1)
            parts.append(jnp.where(lane1 < LEAF - at, a, b))
            off = off + dense_rows(counts_ref[l])
        pot_ref[pl.ds(pl.multiple_of(i * 8, 8), 8), :] = jnp.concatenate(parts, axis=0)
        return off

    lax.fori_loop(0, leaves // 8, place, jnp.int32(0))
    lane = lax.broadcasted_iota(jnp.int32, (leaves, LEAF), 1)
    value = pot_ref[...] * MP ** (-0.5) + near_ref[...]
    pot_ref[...] = jnp.where(lane < column(counts_row_ref[...]), value, 0.0)


def per_device(
    positions, charges, counts, centres, freqs, phases, m2m, m2l, send_nodes, v_source, v_offset, u_source
):
    leaves = counts.shape[0]
    n_gx, n_gy = lax.axis_size("gx"), lax.axis_size("gy")
    devices = n_gx * n_gy
    gy = lax.axis_index("gy").astype(jnp.int32).reshape(1)
    live = jnp.arange(LEAF, dtype=jnp.int32)[None, :] < counts[:, None]
    charge = jnp.where(live, charges.reshape(leaves, LEAF), 0.0)
    stacked = jnp.concatenate([positions.reshape(3 * leaves, LEAF), charge], axis=0)
    up = [(i, i + 1) for i in range(devices - 1)]
    prev = lax.ppermute(stacked, AXES, up)
    after = lax.ppermute(stacked, AXES, [(j, i) for i, j in up])

    counts_row = counts.reshape(1, leaves)
    dense_max = leaves * LEAF
    nodes_dev = leaves + leaves // 8
    limit = pltpu.CompilerParams(vmem_limit_bytes=60 * MIB)
    shape = jax.ShapeDtypeStruct
    vectors = (stacked, counts_row, freqs, phases.reshape(1, MP), send_nodes.reshape(SHIFTS, CAP))
    made = (
        shape((dense_max, MP), BF),
        shape((nodes_dev, MP), BF),
        shape((2 * SHIFTS * CAP, MP), BF),
        shape((REACH * CAP, MP), BF),
    )
    basis, nodes, slots, sel = pl.pallas_call(
        up_kernel,
        grid=(1,),
        out_shape=made,
        in_specs=[SM, SM, SM] + [block(v) for v in vectors] + [HBM],
        out_specs=[HBM] + [block(v) for v in made[1:]],
        scratch_shapes=[
            pltpu.VMEM((dense_max + STEP + LEAF, 32), F32),
            pltpu.VMEM((leaves, MP), F32),
            pltpu.VMEM((2, leaves, LEAF), F32),
            pltpu.VMEM((2, STEP, MP), BF),
            pltpu.VMEM(m2m.shape, BF),
            pltpu.VMEM((SHIFTS * CAP, MP), BF),
            pltpu.SemaphoreType.DMA((3,)),
        ],
        compiler_params=limit,
        cost_estimate=pl.CostEstimate(flops=10**9, bytes_accessed=10**7, transcendentals=4 * 10**6),
        name="upward",
    )(counts, centres.reshape(3 * leaves), gy, *vectors, m2m)

    across = []
    for i in range(devices):
        x, y = i // n_gy, i % n_gy
        to = x + 1 if y >= n_gy // 2 else x - 1
        if 0 <= to < n_gx:
            across.append((i, to * n_gy + y))
    recv = lax.ppermute(sel, AXES, across)

    nearby = (prev, stacked, after, u_source.T)

    def near_part(begin, end, cost):
        return pl.pallas_call(
            functools.partial(near_kernel, begin, end),
            grid=(1,),
            out_shape=shape((end - begin, LEAF), F32),
            in_specs=[SM, SM] + [block(v) for v in nearby],
            out_specs=pl.BlockSpec((end - begin, LEAF), lambda i: (0, 0)),
            scratch_shapes=[
                pltpu.VMEM((3 * leaves * 16, LEAF), BF),
                pltpu.VMEM((3 * leaves * 8, LEAF), F32),
                pltpu.VMEM((leaves * LEAF, 48), BF),
                pltpu.VMEM((leaves * LEAF + NEAR_BIG, LEAF), F32),
                pltpu.SMEM((2 * leaves + 16,), jnp.int32),
                pltpu.SMEM((2 * leaves + 16,), jnp.int32),
            ],
            compiler_params=limit,
            cost_estimate=pl.CostEstimate(flops=cost * 10**9, bytes_accessed=10**6, transcendentals=cost * 10**7),
            name="near",
        )(counts, u_source.T.reshape(leaves * ULIST), *nearby)

    low = (gy[0] < n_gy // 2).astype(jnp.int32)
    slots = lax.dynamic_update_slice(
        slots.reshape(n_gy, 2, CAP, MP), recv.reshape(n_gy // 2, 1, CAP, MP), (low * (n_gy // 2), low, 0, 0)
    )
    got = lax.all_to_all(slots.reshape(n_gy, 2 * CAP, MP), "gy", 0, 0).reshape(2 * SHIFTS * CAP, MP)
    near_all = near_part(0, leaves, 8)

    table_rows = 3 * MP
    vectors = (counts_row, nodes, got, v_source.T, v_offset.T, near_all)
    out = pl.pallas_call(
        down_kernel,
        grid=(1,),
        out_shape=shape((leaves, LEAF), F32),
        in_specs=[SM, SM] + [block(v) for v in vectors] + [HBM, HBM],
        out_specs=block(charge),
        scratch_shapes=[
            pltpu.VMEM((OFFSETS * MP, MP), BF),
            pltpu.VMEM((dense_max, MP), BF),
            pltpu.VMEM((table_rows, MP), BF),
            pltpu.VMEM((leaves, MP), F32),
            pltpu.VMEM((leaves, MP), F32),
            pltpu.VMEM((GROUP * OFFSETS, table_rows), BF),
            pltpu.VMEM((OFFSETS, leaves, MP), BF),
            pltpu.VMEM((leaves, MP), F32),
            pltpu.VMEM((dense_max // LEAF + 8, LEAF), F32),
            pltpu.SemaphoreType.DMA((2,)),
        ],
        compiler_params=limit,
        cost_estimate=pl.CostEstimate(flops=2 * 10**10, bytes_accessed=2 * 10**7, transcendentals=0),
        name="downward",
    )(counts, gy, *vectors, m2l.reshape(OFFSETS * MP, MP), basis)
    return out.reshape(leaves * LEAF)


def solution(mesh):
    both = P(AXES)
    cols = P(None, AXES)
    in_specs = (
        cols, both, both, cols, P(), P(), P(), P(), P(AXES, None, None), P(AXES, None), P(AXES, None), P(AXES, None),
    )
    return jax.shard_map(per_device, mesh=mesh, in_specs=in_specs, out_specs=both, check_vma=False)
```

time: 142 us -> 104 us (0.73); the launches traced: 139 us -> 103 us
  Pallas kernels: 99.9 us -> 75.5 us
  local copies, waits for them, and re-layouts: 15.4 us -> 3.4 us
    pallas_call x4 -> x3, Pallas kernels: 99.9 us -> 75.5 us  [the longest x1 37 us: near_part(): pl.pallas_call(functools.partial(near_kernel, begin, end), grid=(1,), out...]
    unnamed x33 -> x8, local copies, waits for them, and re-layouts: 12.4 us -> 1.63 us
    reshape x3 -> x0, local copies, waits for them, and re-layouts: 1.89 us -> none  [the longest x1 0.95 us: per_device(): send_nodes.reshape(SHIFTS * CAP, 1)]
  transfers between devices with their start and end apart: 4 -> 4, of which waited for: 1 -> 1; matrix products, arithmetic and copies ran while one was open for 3% -> 1% of each run, Pallas kernels for 45% -> 53%
where the time goes in v2:
time: 104 us; the launch traced here: 103 us
  Pallas kernels  75.5 us (73%)
  starting transfers between devices  20 us (19%)
  local copies, waits for them, and re-layouts  3.4 us (3%)
  waiting for transfers between devices  2.82 us (3%)
    pallas_call x1, Pallas kernels, near_part(): pl.pallas_call(functools.partial(near_kernel, begin, end), grid=(1,), out...  37 us
    pallas_call x1, Pallas kernels, per_device(): pl.pallas_call(down_kernel, grid=(1,), out_shape=shape((leaves, LEAF), F3...  21.1 us
    pallas_call x1, Pallas kernels, per_device(): pl.pallas_call(up_kernel, grid=(1,), out_shape=made, in_specs=[SM, SM, SM...  17.5 us
    all_to_all x1, starting transfers between devices, per_device(): lax.all_to_all(slots.reshape(n_gy, 2 * CAP, MP), 'gy', 0, 0)  10.2 us
    ppermute x1, starting transfers between devices, per_device(): after = lax.ppermute(stacked, AXES, [(j, i) for i, j in up])  5.92 us
    ppermute x1, waiting for transfers between devices, per_device(): recv = lax.ppermute(sel, AXES, across)  2.81 us
  transfers between devices with their start and end apart: 4, of which 1 were waited for; matrix products, arithmetic and copies ran while one was open for 1% of the time, Pallas kernels for 53%

profile of v2, /device:TPU:10, one launch (start us, length us, event | category | flops | bytes accessed | tf_op | source)
XLA Modules:
  0.0 102.8 jit_solution(2094769434429028386)
XLA Ops:
  0.0 1.1 %reshape.46 = f32[384,128]{1,0:T(8,128)S(1)} reshape(f32[3,16384]{1,0:T(4,128)} %param.12) | data formatting | bytes 393216 | tf_op jit(solution)/shard_map/reshape | solution.py:424
  1.1 0.9 bitcast_select_fusion
  2.1 0.0 copy-start.1
  2.1 5.9 %collective-permute-start.2 = (f32[512,128]{1,0:T(8,128)S(1)}, f32[512,128]{1,0:T(8,128)S(1)}, u32[]{:S(2)}, u32[]{:S(2)}) collective-permute-start(f32[512,128]{1,0:T(8,128)S(1)} %pad_maximum_fusion.stacked_ref.own_ref), channel_id=1, source_target_pairs={{1,0},{2,1},{3,2},{4,3},{5,4},{6,5},{7,6},{8,7},{9,8},{10,9},{11,1... | collective-permute-start | bytes 786440 | tf_op jit(solution)/shard_map/ppermute | solution.py:427
  8.0 1.9 %collective-permute-start.1 = (f32[512,128]{1,0:T(8,128)S(1)}, f32[512,128]{1,0:T(8,128)S(1)}, u32[]{:S(2)}, u32[]{:S(2)}) collective-permute-start(f32[512,128]{1,0:T(8,128)S(1)} %pad_maximum_fusion.stacked_ref.own_ref), channel_id=1, source_target_pairs={{0,1},{1,2},{2,3},{3,4},{4,5},{5,6},{6,7},{7,8},{8,9},{9,10},{10,1... | collective-permute-start | bytes 786440 | tf_op jit(solution)/shard_map/ppermute | solution.py:426
  9.9 0.0 copy-done.1
  9.9 17.5 %upward.1 = (bf16[16384,256]{1,0:T(8,128)(2,1)}, bf16[144,256]{1,0:T(8,128)(2,1)}, bf16[1024,256]{1,0:T(8,128)(2,1)}, bf16[256,256]{1,0:T(8,128)(2,1)}) custom-call(s32[128]{0:T(128)} %counts_ref.5, f32[384]{0:T(512)} %bitcast.32, s32[1]{0:T(128)} %bitcast.gy_ref, f32[512,128]{1,0:T(8,128)} %copy-done.1, s32[1,128]{1,0:T(1,128)} %bitcast.24, ...), custom_call_target="tpu_custom_call" | custom-call | flops 1000000000 | bytes 10000000 | tf_op jit(solution)/shard_map/upward/pallas_call | solution.py:441
  27.4 1.9 %collective-permute-start = (bf16[256,256]{1,0:T(8,128)(2,1)}, bf16[256,256]{1,0:T(8,128)(2,1)S(1)}, u32[]{:S(2)}, u32[]{:S(2)}) collective-permute-start(bf16[256,256]{1,0:T(8,128)(2,1)} %get-tuple-element.11), channel_id=1, source_target_pairs={{8,24},{9,25},{10,26},{11,27},{12,28},{13,29},{14,30},{15,31},{16,... | collective-permute-start | bytes 393224 | tf_op jit(solution)/shard_map/ppermute | solution.py:467
  29.4 2.8 %collective-permute-done = bf16[256,256]{1,0:T(8,128)(2,1)S(1)} collective-permute-done((bf16[256,256]{1,0:T(8,128)(2,1)}, bf16[256,256]{1,0:T(8,128)(2,1)S(1)}, u32[]{:S(2)}, u32[]{:S(2)}) %collective-permute-start) | collective-permute-done | bytes 131104 | tf_op jit(solution)/shard_map/ppermute | solution.py:467
  32.2 0.7 constant_dynamic-update-slice_fusion
  32.9 10.2 %all-to-all-start = ((bf16[16,64,256]{2,1,0:T(8,128)(2,1)}), bf16[16,64,256]{2,1,0:T(8,128)(2,1)S(1)}, u32[]{:S(2)}, u32[]{:S(2)}) async-start(bf16[16,64,256]{2,1,0:T(8,128)(2,1)} %bitcast.21), calls=%async_computation | async-start | bytes 1048576 | tf_op jit(solution)/shard_map/all_to_all | solution.py:495
  43.1 0.0 collective-permute-done.2.next_ref
  43.1 0.0 copy-start.2
  43.1 0.0 collective-permute-done.1.prev_ref
  43.1 0.0 copy-start.3
  43.1 0.7 copy-done.2
  43.8 0.1 copy-done.3
  43.9 37.0 %near.1.near_ref = f32[128,128]{1,0:T(8,128)} custom-call(s32[128]{0:T(128)} %counts_ref.5, s32[3456]{0:T(1024)} %bitcast.29, f32[512,128]{1,0:T(8,128)} %copy-done.3, f32[512,128]{1,0:T(8,128)} %copy-done.1, f32[512,128]{1,0:T(8,128)} %copy-done.2, s32[27,128]{1,0:T(8,128)} %bitcast.30), custom_call_target="tpu_custom_call" | custom-call | flops 8000000000 | bytes 1000000 | tf_op jit(solution)/shard_map/near/pallas_call | solution.py:472
  80.9 0.0 all-to-all-done
  80.9 0.0 copy-start
  80.9 0.8 copy-done
  81.7 21.1 %downward.1 = f32[128,128]{1,0:T(8,128)} custom-call(s32[128]{0:T(128)} %counts_ref.5, s32[1]{0:T(128)} %bitcast.gy_ref, s32[1,128]{1,0:T(1,128)} %bitcast.25, bf16[144,256]{1,0:T(8,128)(2,1)} %get-tuple-element.9.nodes_ref, bf16[1024,256]{1,0:T(8,128)(2,1)} %bitcast.22, s32[189,128]{1,0:T(8,128)} %bitcast.27, s32[189,128]{1,0:T(8,128)} %bitcast.28, ...), custom_call_target="tpu_custom_call" | custom-call | flops 20000000000 | bytes 20000000 | tf_op jit(solution)/shard_map/downward/pallas_call | solution.py:500
  (1 shorter events, 0.0 us)
Async XLA Ops:
  2.1 7.9 %copy-start.1 = (f32[512,128]{1,0:T(8,128)}, f32[512,128]{1,0:T(8,128)S(1)}, u32[]{:S(2)}) copy-start(f32[512,128]{1,0:T(8,128)S(1)} %pad_maximum_fusion.stacked_ref.own_ref) | copy-start | bytes 786436
  2.1 41.0 %collective-permute-start.2 = (f32[512,128]{1,0:T(8,128)S(1)}, f32[512,128]{1,0:T(8,128)S(1)}, u32[]{:S(2)}, u32[]{:S(2)}) collective-permute-start(f32[512,128]{1,0:T(8,128)S(1)} %pad_maximum_fusion.stacked_ref.own_ref), channel_id=1, source_target_pairs={{1,0},{2,1},{3,2},{4,3},{5,4},{6,5},{7,6},{8,7},{9,8},{10,9},{11,1... | collective-permute-start | bytes 786440 | tf_op jit(solution)/shard_map/ppermute | solution.py:427
  8.0 35.1 %collective-permute-start.1 = (f32[512,128]{1,0:T(8,128)S(1)}, f32[512,128]{1,0:T(8,128)S(1)}, u32[]{:S(2)}, u32[]{:S(2)}) collective-permute-start(f32[512,128]{1,0:T(8,128)S(1)} %pad_maximum_fusion.stacked_ref.own_ref), channel_id=1, source_target_pairs={{0,1},{1,2},{2,3},{3,4},{4,5},{5,6},{6,7},{7,8},{8,9},{9,10},{10,1... | collective-permute-start | bytes 786440 | tf_op jit(solution)/shard_map/ppermute | solution.py:426
  27.4 4.7 %collective-permute-start = (bf16[256,256]{1,0:T(8,128)(2,1)}, bf16[256,256]{1,0:T(8,128)(2,1)S(1)}, u32[]{:S(2)}, u32[]{:S(2)}) collective-permute-start(bf16[256,256]{1,0:T(8,128)(2,1)} %get-tuple-element.11), channel_id=1, source_target_pairs={{8,24},{9,25},{10,26},{11,27},{12,28},{13,29},{14,30},{15,31},{16,... | collective-permute-start | bytes 393224 | tf_op jit(solution)/shard_map/ppermute | solution.py:467
  32.9 48.0 %all-to-all-start = ((bf16[16,64,256]{2,1,0:T(8,128)(2,1)}), bf16[16,64,256]{2,1,0:T(8,128)(2,1)S(1)}, u32[]{:S(2)}, u32[]{:S(2)}) async-start(bf16[16,64,256]{2,1,0:T(8,128)(2,1)} %bitcast.21), calls=%async_computation | async-start | bytes 1048576 | tf_op jit(solution)/shard_map/all_to_all | solution.py:495
  43.1 0.7 copy-start.2
  43.1 0.8 copy-start.3
  80.9 0.8 copy-start

commit v3 on v2

--- a/solution.py
+++ b/solution.py
@@ -208,7 +208,7 @@
 
 
 def near_kernel(
-    begin, end, counts_ref, us_ref, prev_ref, own_ref, next_ref, usv_ref,
+    begin, end, counts_ref, odd_ref, us_ref, evens_ref, own_ref, odds_ref, usv_ref,
     near_ref, feat, charge, tgt, acc_ref, big, small,
 ):
     leaves = own_ref.shape[0] // 4
@@ -217,7 +217,8 @@
     def coords(ref, l):
         return [jnp.broadcast_to(ref[pl.ds(c * leaves + l, 1), :] - 2.0, (8, LEAF)) for c in range(3)]
 
-    for part, ref in enumerate((prev_ref, own_ref, next_ref)):
+    odd = odd_ref[0]
+    for part, ref in ((2 * (1 - odd), evens_ref), (1, own_ref), (2 * odd, odds_ref)):
 
         def build(i, _, part=part, ref=ref):
             for k in range(8):
@@ -228,8 +229,8 @@
                 a = jnp.where(rows < 3, s1, jnp.where(rows < 6, s2, jnp.where(rows == 6, n1, n2)))
                 b = jnp.where(rows < 3, s3, jnp.where(rows == 3, n3, 1.0))
                 s = part * leaves + l
-                feat[pl.ds(pl.multiple_of(s * 16, 16), 16), :] = jnp.concatenate([a, b], axis=0).astype(BF)
-                charge[pl.ds(pl.multiple_of(s * 8, 8), 8), :] = jnp.broadcast_to(
+                feat[s] = jnp.concatenate([a, b], axis=0).astype(BF)
+                charge[s] = jnp.broadcast_to(
                     ref[pl.ds(3 * leaves + l, 1), :], (8, LEAF)
                 )
             return 0
@@ -266,7 +267,7 @@
             m = m + ((left > 0) & (left <= NEAR_SMALL)).astype(jnp.int32)
         return n, m
 
-    n_big, n_small = lax.fori_loop(begin, end, listing, (jnp.int32(0), jnp.int32(0)))
+    n_big, n_small = lax.fori_loop(begin, end, listing, (jnp.int32(0), jnp.int32(0)), unroll=4)
 
     def run(items, n, size, unroll):
         for k in range(unroll):
@@ -281,11 +282,11 @@
                 acc = None
                 for u in range(0, ULIST, 2):
                     two = [us_ref[v * leaves + l] for v in range(u, min(u + 2, ULIST))]
-                    f = [feat[pl.ds(pl.multiple_of(s * 16, 16), 16), :] for s in two]
+                    f = [feat[s] for s in two]
                     f = jnp.concatenate(f, axis=1) if len(f) > 1 else f[0]
                     r = lax.rsqrt(dot(lhs, jnp.concatenate([f, f, f], axis=0)))
                     for j, s in enumerate(two):
-                        q = charge[pl.ds(pl.multiple_of(s * 8, 8), 8), :]
+                        q = charge[s]
                         term = r[:, j * LEAF:(j + 1) * LEAF].reshape(size // 8, 8, LEAF) * q[None]
                         acc = term if acc is None else acc + term
                 acc_ref[pl.ds(pl.multiple_of(place, NEAR_SMALL), size), :] = acc.reshape(size, LEAF)
@@ -422,9 +423,12 @@
     live = jnp.arange(LEAF, dtype=jnp.int32)[None, :] < counts[:, None]
     charge = jnp.where(live, charges.reshape(leaves, LEAF), 0.0)
     stacked = jnp.concatenate([positions.reshape(3 * leaves, LEAF), charge], axis=0)
-    up = [(i, i + 1) for i in range(devices - 1)]
-    prev = lax.ppermute(stacked, AXES, up)
-    after = lax.ppermute(stacked, AXES, [(j, i) for i, j in up])
+    def swapped(first):
+        lower = range(first, devices - 1, 2)
+        return lax.ppermute(stacked, AXES, [(i, i + 1) for i in lower] + [(i + 1, i) for i in lower])
+
+    evens, odds = swapped(0), swapped(1)
+    odd = gy & 1
 
     counts_row = counts.reshape(1, leaves)
     dense_max = leaves * LEAF
@@ -466,18 +470,18 @@
             across.append((i, to * n_gy + y))
     recv = lax.ppermute(sel, AXES, across)
 
-    nearby = (prev, stacked, after, u_source.T)
+    nearby = (evens, stacked, odds, u_source.T)
 
     def near_part(begin, end, cost):
         return pl.pallas_call(
             functools.partial(near_kernel, begin, end),
             grid=(1,),
             out_shape=shape((end - begin, LEAF), F32),
-            in_specs=[SM, SM] + [block(v) for v in nearby],
+            in_specs=[SM, SM, SM] + [block(v) for v in nearby],
             out_specs=pl.BlockSpec((end - begin, LEAF), lambda i: (0, 0)),
             scratch_shapes=[
-                pltpu.VMEM((3 * leaves * 16, LEAF), BF),
-                pltpu.VMEM((3 * leaves * 8, LEAF), F32),
+                pltpu.VMEM((3 * leaves, 16, LEAF), BF),
+                pltpu.VMEM((3 * leaves, 8, LEAF), F32),
                 pltpu.VMEM((leaves * LEAF, 48), BF),
                 pltpu.VMEM((leaves * LEAF + NEAR_BIG, LEAF), F32),
                 pltpu.SMEM((2 * leaves + 16,), jnp.int32),
@@ -486,7 +490,7 @@
             compiler_params=limit,
             cost_estimate=pl.CostEstimate(flops=cost * 10**9, bytes_accessed=10**6, transcendentals=cost * 10**7),
             name="near",
-        )(counts, u_source.T.reshape(leaves * ULIST), *nearby)
+        )(counts, odd, u_source.T.reshape(leaves * ULIST), *nearby)
 
     low = (gy[0] < n_gy // 2).astype(jnp.int32)
     slots = lax.dynamic_update_slice(

time: 104 us -> 99.9 us (0.961)
  the two profiles are of different devices: /device:TPU:10 before, /device:TPU:49 now
where the time goes in v3:
time: 99.9 us; the launch traced here: 100 us
  Pallas kernels  77.4 us (77%)
  starting transfers between devices  13.7 us (14%)
  waiting for transfers between devices  4.57 us (5%)
  local copies, waits for them, and re-layouts  3.4 us (3%)
    pallas_call x1, Pallas kernels, near_part(): pl.pallas_call(functools.partial(near_kernel, begin, end), grid=(1,), out...  37.3 us
    pallas_call x1, Pallas kernels, per_device(): pl.pallas_call(down_kernel, grid=(1,), out_shape=shape((leaves, LEAF), F3...  21.4 us
    pallas_call x1, Pallas kernels, per_device(): pl.pallas_call(up_kernel, grid=(1,), out_shape=made, in_specs=[SM, SM, SM...  18.7 us
    ppermute x2, starting transfers between devices, swapped(): lax.ppermute(stacked, AXES, [(i, i + 1) for i in lower] + [(i + 1, i) for...  8.33 us
    ppermute x1, waiting for transfers between devices, per_device(): recv = lax.ppermute(sel, AXES, across)  4.56 us
    all_to_all x1, starting transfers between devices, per_device(): lax.all_to_all(slots.reshape(n_gy, 2 * CAP, MP), 'gy', 0, 0)  3.47 us
  transfers between devices with their start and end apart: 4, of which 1 were waited for; matrix products, arithmetic and copies ran while one was open for 1% of the time, Pallas kernels for 56%

profile of v3, /device:TPU:49, one launch (start us, length us, event | category | flops | bytes accessed | tf_op | source)
XLA Modules:
  0.0 100.2 jit_solution(11433847328573909421)
XLA Ops:
  0.0 1.1 %reshape.46 = f32[384,128]{1,0:T(8,128)S(1)} reshape(f32[3,16384]{1,0:T(4,128)} %param.12) | data formatting | bytes 393216 | tf_op jit(solution)/shard_map/reshape | solution.py:425
  1.1 0.9 bitcast_select_fusion
  2.1 0.0 copy-start.1
  2.1 3.5 %collective-permute-start.2 = (f32[512,128]{1,0:T(8,128)S(1)}, f32[512,128]{1,0:T(8,128)S(1)}, u32[]{:S(2)}, u32[]{:S(2)}) collective-permute-start(f32[512,128]{1,0:T(8,128)S(1)} %pad_maximum_fusion.stacked_ref.own_ref), channel_id=1, source_target_pairs={{1,2},{3,4},{5,6},{7,8},{9,10},{11,12},{13,14},{15,16},{17,18},{19... | collective-permute-start | bytes 786440 | tf_op jit(solution)/shard_map/ppermute | solution.py:428
  5.6 4.8 %collective-permute-start.1 = (f32[512,128]{1,0:T(8,128)S(1)}, f32[512,128]{1,0:T(8,128)S(1)}, u32[]{:S(2)}, u32[]{:S(2)}) collective-permute-start(f32[512,128]{1,0:T(8,128)S(1)} %pad_maximum_fusion.stacked_ref.own_ref), channel_id=1, source_target_pairs={{0,1},{2,3},{4,5},{6,7},{8,9},{10,11},{12,13},{14,15},{16,17},{18,... | collective-permute-start | bytes 786440 | tf_op jit(solution)/shard_map/ppermute | solution.py:428
  10.4 0.0 copy-done.1
  10.4 18.7 %upward.1 = (bf16[16384,256]{1,0:T(8,128)(2,1)}, bf16[144,256]{1,0:T(8,128)(2,1)}, bf16[1024,256]{1,0:T(8,128)(2,1)}, bf16[256,256]{1,0:T(8,128)(2,1)}) custom-call(s32[128]{0:T(128)} %counts_ref.5, f32[384]{0:T(512)} %bitcast.32, s32[1]{0:T(128)} %bitcast.gy_ref, f32[512,128]{1,0:T(8,128)} %copy-done.1, s32[1,128]{1,0:T(1,128)} %bitcast.24, ...), custom_call_target="tpu_custom_call" | custom-call | flops 1000000000 | bytes 10000000 | tf_op jit(solution)/shard_map/upward/pallas_call | solution.py:445
  29.1 1.9 %collective-permute-start = (bf16[256,256]{1,0:T(8,128)(2,1)}, bf16[256,256]{1,0:T(8,128)(2,1)S(1)}, u32[]{:S(2)}, u32[]{:S(2)}) collective-permute-start(bf16[256,256]{1,0:T(8,128)(2,1)} %get-tuple-element.11), channel_id=1, source_target_pairs={{8,24},{9,25},{10,26},{11,27},{12,28},{13,29},{14,30},{15,31},{16,... | collective-permute-start | bytes 393224 | tf_op jit(solution)/shard_map/ppermute | solution.py:471
  31.1 4.6 %collective-permute-done = bf16[256,256]{1,0:T(8,128)(2,1)S(1)} collective-permute-done((bf16[256,256]{1,0:T(8,128)(2,1)}, bf16[256,256]{1,0:T(8,128)(2,1)S(1)}, u32[]{:S(2)}, u32[]{:S(2)}) %collective-permute-start) | collective-permute-done | bytes 131104 | tf_op jit(solution)/shard_map/ppermute | solution.py:471
  35.6 0.7 constant_dynamic-update-slice_fusion
  36.3 3.5 %all-to-all-start = ((bf16[16,64,256]{2,1,0:T(8,128)(2,1)}), bf16[16,64,256]{2,1,0:T(8,128)(2,1)S(1)}, u32[]{:S(2)}, u32[]{:S(2)}) async-start(bf16[16,64,256]{2,1,0:T(8,128)(2,1)} %bitcast.21), calls=%async_computation | async-start | bytes 1048576 | tf_op jit(solution)/shard_map/all_to_all | solution.py:499
  39.8 0.0 collective-permute-done.2.odds_ref
  39.8 0.0 copy-start.2
  39.8 0.0 collective-permute-done.1.evens_ref
  39.8 0.0 copy-start.3
  39.8 0.7 copy-done.2
  40.5 0.1 copy-done.3
  40.6 37.3 %near.1.near_ref = f32[128,128]{1,0:T(8,128)} custom-call(s32[128]{0:T(128)} %counts_ref.5, s32[1]{0:T(128)S(6)} %and.4.odd_ref, s32[3456]{0:T(1024)} %bitcast.29, f32[512,128]{1,0:T(8,128)} %copy-done.3, f32[512,128]{1,0:T(8,128)} %copy-done.1, f32[512,128]{1,0:T(8,128)} %copy-done.2, s32[27,128]{1,0:T(8,128)} %bitcast.30), custom_call_target="tpu_custom_call" | custom-call | flops 8000000000 | bytes 1000000 | tf_op jit(solution)/shard_map/near/pallas_call | solution.py:476
  77.9 0.0 all-to-all-done
  77.9 0.0 copy-start
  77.9 0.8 copy-done
  78.7 21.4 %downward.1 = f32[128,128]{1,0:T(8,128)} custom-call(s32[128]{0:T(128)} %counts_ref.5, s32[1]{0:T(128)} %bitcast.gy_ref, s32[1,128]{1,0:T(1,128)} %bitcast.25, bf16[144,256]{1,0:T(8,128)(2,1)} %get-tuple-element.9.nodes_ref, bf16[1024,256]{1,0:T(8,128)(2,1)} %bitcast.22, s32[189,128]{1,0:T(8,128)} %bitcast.27, s32[189,128]{1,0:T(8,128)} %bitcast.28, ...), custom_call_target="tpu_custom_call" | custom-call | flops 20000000000 | bytes 20000000 | tf_op jit(solution)/shard_map/downward/pallas_call | solution.py:504
  (1 shorter events, 0.0 us)
Async XLA Ops:
  2.1 8.3 %copy-start.1 = (f32[512,128]{1,0:T(8,128)}, f32[512,128]{1,0:T(8,128)S(1)}, u32[]{:S(2)}) copy-start(f32[512,128]{1,0:T(8,128)S(1)} %pad_maximum_fusion.stacked_ref.own_ref) | copy-start | bytes 786436
  2.1 37.7 %collective-permute-start.2 = (f32[512,128]{1,0:T(8,128)S(1)}, f32[512,128]{1,0:T(8,128)S(1)}, u32[]{:S(2)}, u32[]{:S(2)}) collective-permute-start(f32[512,128]{1,0:T(8,128)S(1)} %pad_maximum_fusion.stacked_ref.own_ref), channel_id=1, source_target_pairs={{1,2},{3,4},{5,6},{7,8},{9,10},{11,12},{13,14},{15,16},{17,18},{19... | collective-permute-start | bytes 786440 | tf_op jit(solution)/shard_map/ppermute | solution.py:428
  5.6 34.2 %collective-permute-start.1 = (f32[512,128]{1,0:T(8,128)S(1)}, f32[512,128]{1,0:T(8,128)S(1)}, u32[]{:S(2)}, u32[]{:S(2)}) collective-permute-start(f32[512,128]{1,0:T(8,128)S(1)} %pad_maximum_fusion.stacked_ref.own_ref), channel_id=1, source_target_pairs={{0,1},{2,3},{4,5},{6,7},{8,9},{10,11},{12,13},{14,15},{16,17},{18,... | collective-permute-start | bytes 786440 | tf_op jit(solution)/shard_map/ppermute | solution.py:428
  29.1 6.5 %collective-permute-start = (bf16[256,256]{1,0:T(8,128)(2,1)}, bf16[256,256]{1,0:T(8,128)(2,1)S(1)}, u32[]{:S(2)}, u32[]{:S(2)}) collective-permute-start(bf16[256,256]{1,0:T(8,128)(2,1)} %get-tuple-element.11), channel_id=1, source_target_pairs={{8,24},{9,25},{10,26},{11,27},{12,28},{13,29},{14,30},{15,31},{16,... | collective-permute-start | bytes 393224 | tf_op jit(solution)/shard_map/ppermute | solution.py:471
  36.3 41.6 %all-to-all-start = ((bf16[16,64,256]{2,1,0:T(8,128)(2,1)}), bf16[16,64,256]{2,1,0:T(8,128)(2,1)S(1)}, u32[]{:S(2)}, u32[]{:S(2)}) async-start(bf16[16,64,256]{2,1,0:T(8,128)(2,1)} %bitcast.21), calls=%async_computation | async-start | bytes 1048576 | tf_op jit(solution)/shard_map/all_to_all | solution.py:499
  39.8 0.7 copy-start.2
  39.8 0.8 copy-start.3
  77.9 0.8 copy-start

commit v4 on v3

--- a/solution.py
+++ b/solution.py
@@ -22,7 +22,7 @@
 SHIFTS = 16
 AXES = ("gx", "gy")
 ROWS = 256
-STEP = 512
+STEP = 1024
 MIB = 2**20
 SM = pl.BlockSpec(memory_space=pltpu.SMEM)
 HBM = pl.BlockSpec(memory_space=pl.ANY)
@@ -157,7 +157,7 @@
             lo = (w - hi.astype(F32)).astype(BF)
             member = ((lane >= first - base) & (lane < last - base)).astype(F32).astype(BF)
             sums.append(dot(member, hi) + dot(member, lo))
-        total[...] += sums[0] + sums[1]
+        total[...] += sum(sums)
         written(i, slot).start()
         return 0
 
@@ -299,14 +299,14 @@
 
     def reduce(i, _):
         parts = []
-        for k in range(8):
-            l = i * 8 + k
+        for k in range(16):
+            l = i * 16 + k
             t = acc_ref[pl.ds(pl.multiple_of(l * LEAF, LEAF), LEAF), :].T
             parts.append(jnp.sum(t, axis=0, keepdims=True))
-        near_ref[pl.ds(pl.multiple_of(i * 8 - begin, 8), 8), :] = jnp.concatenate(parts, axis=0)
+        near_ref[pl.ds(pl.multiple_of(i * 16 - begin, 16), 16), :] = jnp.concatenate(parts, axis=0)
         return 0
 
-    lax.fori_loop(begin // 8, end // 8, reduce, 0)
+    lax.fori_loop(begin // 16, end // 16, reduce, 0)
     own_id = lax.broadcasted_iota(jnp.int32, usv_ref.shape, 1) + leaves
     times = column(jnp.sum((usv_ref[...] == own_id).astype(F32), axis=0, keepdims=True)).astype(F32)
     itself = own_ref[3 * leaves + begin:3 * leaves + end, :] * lax.rsqrt(jnp.full((1, LEAF), 0.01, F32))
@@ -366,11 +366,11 @@
     local[...] = jnp.zeros_like(local)
 
     def translate(i, _):
-        parts = [summed[i * 8 + k] for k in range(8)]
-        local[...] += dot(jnp.concatenate(parts, axis=1), m2l[pl.ds(pl.multiple_of(i * 8 * MP, 8 * MP), 8 * MP), :])
+        parts = [summed[i * 16 + k] for k in range(16)]
+        local[...] += dot(jnp.concatenate(parts, axis=1), m2l[pl.ds(pl.multiple_of(i * 16 * MP, 16 * MP), 16 * MP), :])
         return 0
 
-    lax.fori_loop(0, OFFSETS // 8, translate, 0)
+    lax.fori_loop(0, OFFSETS // 16, translate, 0)
     hi = local[...].astype(BF)
     lo = (local[...] - hi.astype(F32)).astype(BF)
     both = jnp.concatenate([hi, lo], axis=0)
@@ -396,18 +396,18 @@
 
     def place(i, off):
         parts = []
-        for k in range(8):
-            l = i * 8 + k
+        for k in range(16):
+            l = i * 16 + k
             row, at = off >> 7, off & (LEAF - 1)
             shift = (LEAF - at) & (LEAF - 1)
             a = pltpu.roll(far[pl.ds(row, 1), :], shift, 1)
             b = pltpu.roll(far[pl.ds(row + 1, 1), :], shift, 1)
             parts.append(jnp.where(lane1 < LEAF - at, a, b))
             off = off + dense_rows(counts_ref[l])
-        pot_ref[pl.ds(pl.multiple_of(i * 8, 8), 8), :] = jnp.concatenate(parts, axis=0)
+        pot_ref[pl.ds(pl.multiple_of(i * 16, 16), 16), :] = jnp.concatenate(parts, axis=0)
         return off
 
-    lax.fori_loop(0, leaves // 8, place, jnp.int32(0))
+    lax.fori_loop(0, leaves // 16, place, jnp.int32(0))
     lane = lax.broadcasted_iota(jnp.int32, (leaves, LEAF), 1)
     value = pot_ref[...] * MP ** (-0.5) + near_ref[...]
     pot_ref[...] = jnp.where(lane < column(counts_row_ref[...]), value, 0.0)

time: 99.9 us -> 95.1 us (0.952)
  the two profiles are of different devices: /device:TPU:49 before, /device:TPU:26 now
where the time goes in v4:
time: 95.1 us; the launch traced here: 93.7 us
  Pallas kernels  71.4 us (75%)
  starting transfers between devices  15 us (16%)
  local copies, waits for them, and re-layouts  3.4 us (4%)
  waiting for transfers between devices  2.82 us (3%)
    pallas_call x1, Pallas kernels, near_part(): pl.pallas_call(functools.partial(near_kernel, begin, end), grid=(1,), out...  35.2 us
    pallas_call x1, Pallas kernels, per_device(): pl.pallas_call(down_kernel, grid=(1,), out_shape=shape((leaves, LEAF), F3...  20.2 us
    pallas_call x1, Pallas kernels, per_device(): pl.pallas_call(up_kernel, grid=(1,), out_shape=made, in_specs=[SM, SM, SM...  16 us
    all_to_all x1, starting transfers between devices, per_device(): lax.all_to_all(slots.reshape(n_gy, 2 * CAP, MP), 'gy', 0, 0)  7.1 us
    ppermute x2, starting transfers between devices, swapped(): lax.ppermute(stacked, AXES, [(i, i + 1) for i in lower] + [(i + 1, i) for...  6 us
    ppermute x1, waiting for transfers between devices, per_device(): recv = lax.ppermute(sel, AXES, across)  2.81 us
    ppermute x1, starting transfers between devices, per_device(): recv = lax.ppermute(sel, AXES, across)  1.92 us
  transfers between devices with their start and end apart: 4, of which 1 were waited for; matrix products, arithmetic and copies ran while one was open for 1% of the time, Pallas kernels for 55%

profile of v4, /device:TPU:26, one launch (start us, length us, event | category | flops | bytes accessed | tf_op | source)
XLA Modules:
  0.0 93.7 jit_solution(6590615077655632916)
XLA Ops:
  0.0 1.1 %reshape.46 = f32[384,128]{1,0:T(8,128)S(1)} reshape(f32[3,16384]{1,0:T(4,128)} %param.12) | data formatting | bytes 393216 | tf_op jit(solution)/shard_map/reshape | solution.py:425
  1.1 0.9 bitcast_select_fusion
  2.1 0.0 copy-start.1
  2.1 5.9 %collective-permute-start.2 = (f32[512,128]{1,0:T(8,128)S(1)}, f32[512,128]{1,0:T(8,128)S(1)}, u32[]{:S(2)}, u32[]{:S(2)}) collective-permute-start(f32[512,128]{1,0:T(8,128)S(1)} %pad_maximum_fusion.stacked_ref.own_ref), channel_id=1, source_target_pairs={{1,2},{3,4},{5,6},{7,8},{9,10},{11,12},{13,14},{15,16},{17,18},{19... | collective-permute-start | bytes 786440 | tf_op jit(solution)/shard_map/ppermute | solution.py:428
  8.0 0.1 collective-permute-start.1
  8.1 0.0 copy-done.1
  8.1 16.0 %upward.1 = (bf16[16384,256]{1,0:T(8,128)(2,1)}, bf16[144,256]{1,0:T(8,128)(2,1)}, bf16[1024,256]{1,0:T(8,128)(2,1)}, bf16[256,256]{1,0:T(8,128)(2,1)}) custom-call(s32[128]{0:T(128)} %counts_ref.5, f32[384]{0:T(512)} %bitcast.32, s32[1]{0:T(128)} %bitcast.gy_ref, f32[512,128]{1,0:T(8,128)} %copy-done.1, s32[1,128]{1,0:T(1,128)} %bitcast.24, ...), custom_call_target="tpu_custom_call" | custom-call | flops 1000000000 | bytes 10000000 | tf_op jit(solution)/shard_map/upward/pallas_call | solution.py:445
  24.1 1.9 %collective-permute-start = (bf16[256,256]{1,0:T(8,128)(2,1)}, bf16[256,256]{1,0:T(8,128)(2,1)S(1)}, u32[]{:S(2)}, u32[]{:S(2)}) collective-permute-start(bf16[256,256]{1,0:T(8,128)(2,1)} %get-tuple-element.11), channel_id=1, source_target_pairs={{8,24},{9,25},{10,26},{11,27},{12,28},{13,29},{14,30},{15,31},{16,... | collective-permute-start | bytes 393224 | tf_op jit(solution)/shard_map/ppermute | solution.py:471
  26.0 2.8 %collective-permute-done = bf16[256,256]{1,0:T(8,128)(2,1)S(1)} collective-permute-done((bf16[256,256]{1,0:T(8,128)(2,1)}, bf16[256,256]{1,0:T(8,128)(2,1)S(1)}, u32[]{:S(2)}, u32[]{:S(2)}) %collective-permute-start) | collective-permute-done | bytes 131104 | tf_op jit(solution)/shard_map/ppermute | solution.py:471
  28.8 0.7 constant_dynamic-update-slice_fusion
  29.5 7.1 %all-to-all-start = ((bf16[16,64,256]{2,1,0:T(8,128)(2,1)}), bf16[16,64,256]{2,1,0:T(8,128)(2,1)S(1)}, u32[]{:S(2)}, u32[]{:S(2)}) async-start(bf16[16,64,256]{2,1,0:T(8,128)(2,1)} %bitcast.21), calls=%async_computation | async-start | bytes 1048576 | tf_op jit(solution)/shard_map/all_to_all | solution.py:499
  36.6 0.0 collective-permute-done.2.odds_ref
  36.6 0.0 copy-start.2
  36.6 0.0 collective-permute-done.1.evens_ref
  36.6 0.0 copy-start.3
  36.6 0.7 copy-done.2
  37.3 0.1 copy-done.3
  37.4 35.2 %near.1.near_ref = f32[128,128]{1,0:T(8,128)} custom-call(s32[128]{0:T(128)} %counts_ref.5, s32[1]{0:T(128)S(6)} %and.4.odd_ref, s32[3456]{0:T(1024)} %bitcast.29, f32[512,128]{1,0:T(8,128)} %copy-done.3, f32[512,128]{1,0:T(8,128)} %copy-done.1, f32[512,128]{1,0:T(8,128)} %copy-done.2, s32[27,128]{1,0:T(8,128)} %bitcast.30), custom_call_target="tpu_custom_call" | custom-call | flops 8000000000 | bytes 1000000 | tf_op jit(solution)/shard_map/near/pallas_call | solution.py:476
  72.6 0.0 all-to-all-done
  72.6 0.0 copy-start
  72.6 0.8 copy-done
  73.5 20.2 %downward.1 = f32[128,128]{1,0:T(8,128)} custom-call(s32[128]{0:T(128)} %counts_ref.5, s32[1]{0:T(128)} %bitcast.gy_ref, s32[1,128]{1,0:T(1,128)} %bitcast.25, bf16[144,256]{1,0:T(8,128)(2,1)} %get-tuple-element.9.nodes_ref, bf16[1024,256]{1,0:T(8,128)(2,1)} %bitcast.22, s32[189,128]{1,0:T(8,128)} %bitcast.27, s32[189,128]{1,0:T(8,128)} %bitcast.28, ...), custom_call_target="tpu_custom_call" | custom-call | flops 20000000000 | bytes 20000000 | tf_op jit(solution)/shard_map/downward/pallas_call | solution.py:504
  (1 shorter events, 0.0 us)
Async XLA Ops:
  2.1 6.0 %copy-start.1 = (f32[512,128]{1,0:T(8,128)}, f32[512,128]{1,0:T(8,128)S(1)}, u32[]{:S(2)}) copy-start(f32[512,128]{1,0:T(8,128)S(1)} %pad_maximum_fusion.stacked_ref.own_ref) | copy-start | bytes 786436
  2.1 34.5 %collective-permute-start.2 = (f32[512,128]{1,0:T(8,128)S(1)}, f32[512,128]{1,0:T(8,128)S(1)}, u32[]{:S(2)}, u32[]{:S(2)}) collective-permute-start(f32[512,128]{1,0:T(8,128)S(1)} %pad_maximum_fusion.stacked_ref.own_ref), channel_id=1, source_target_pairs={{1,2},{3,4},{5,6},{7,8},{9,10},{11,12},{13,14},{15,16},{17,18},{19... | collective-permute-start | bytes 786440 | tf_op jit(solution)/shard_map/ppermute | solution.py:428
  8.0 28.6 %collective-permute-start.1 = (f32[512,128]{1,0:T(8,128)S(1)}, f32[512,128]{1,0:T(8,128)S(1)}, u32[]{:S(2)}, u32[]{:S(2)}) collective-permute-start(f32[512,128]{1,0:T(8,128)S(1)} %pad_maximum_fusion.stacked_ref.own_ref), channel_id=1, source_target_pairs={{0,1},{2,3},{4,5},{6,7},{8,9},{10,11},{12,13},{14,15},{16,17},{18,... | collective-permute-start | bytes 786440 | tf_op jit(solution)/shard_map/ppermute | solution.py:428
  24.1 4.7 %collective-permute-start = (bf16[256,256]{1,0:T(8,128)(2,1)}, bf16[256,256]{1,0:T(8,128)(2,1)S(1)}, u32[]{:S(2)}, u32[]{:S(2)}) collective-permute-start(bf16[256,256]{1,0:T(8,128)(2,1)} %get-tuple-element.11), channel_id=1, source_target_pairs={{8,24},{9,25},{10,26},{11,27},{12,28},{13,29},{14,30},{15,31},{16,... | collective-permute-start | bytes 393224 | tf_op jit(solution)/shard_map/ppermute | solution.py:471
  29.5 43.1 %all-to-all-start = ((bf16[16,64,256]{2,1,0:T(8,128)(2,1)}), bf16[16,64,256]{2,1,0:T(8,128)(2,1)S(1)}, u32[]{:S(2)}, u32[]{:S(2)}) async-start(bf16[16,64,256]{2,1,0:T(8,128)(2,1)} %bitcast.21), calls=%async_computation | async-start | bytes 1048576 | tf_op jit(solution)/shard_map/all_to_all | solution.py:499
  36.6 0.7 copy-start.2
  36.6 0.8 copy-start.3
  72.6 0.8 copy-start
